TPU v7x, 512 devices: a whole 4x4x16 slice. The times are simulated.
512 devices in a mesh: section: 16 (over y_lo, x, core), expert: 32 (over y_hi, z).
Axes of the slice: x: 4, y: 4 (y_hi: 2, y_lo: 2; y = y_hi * 2 + y_lo), z: 16, core: 2. Of those that a mesh axis runs over, the one named last changes fastest.
Arguments:
- tokens: bfloat16 [8192, 7168], P('expert', 'section'), may hold values from -6 to 6
- grad_out: bfloat16 [8192, 7168], P('expert', 'section'), may hold values from -6 to 6
- expert_ids: int32 [8192, 8], P('expert'), may hold values from 0 to 255, all different within a row; in each aligned block of 256 rows (0 to 255, 256 to 511, ...) at most 12 rows name the same one
- route_weight: float32 [8192, 8], P('expert'), may hold values from 0.1 to 1
- up_weight: bfloat16 [32, 7168, 2048], P('expert', 'section'), may hold values from -0.0625 to 0.0625
- down_weight: bfloat16 [32, 2048, 7168], P('expert', None, 'section'), may hold values from -0.125 to 0.125
Outputs:
- mixed: bfloat16 [8192, 7168], P('expert', 'section')
- grad_tokens: bfloat16 [8192, 7168], P('expert', 'section')
Inputs may be any that keep to these rules, and one draw needn't show every extreme that they name: `expert_ids`: in each aligned block of 256 tokens (the rows of one device) no expert number is named by more than 12 routes, and a row names 8 different numbers. Numbers from 32 on belong to experts held elsewhere.
All inputs are finite; a program needn't handle non-finite values.
Results may differ from a plain program's by a relative error of at most 0.029.
Values may be sent and summed in bfloat16 or wider, within the bound.
No kernel may reach another device: no remote copies, remote signals or barrier semaphores. Data moves between devices by JAX's collectives and lax.ppermute only.
A program may use at most 64 MiB of HBM per device.

v0:
```python
import jax
import jax.numpy as jnp
from jax import lax
from jax.sharding import PartitionSpec as P

CAP = 12


def expert_rows(rows_x, rows_dy, up_matrix, down_matrix):
    up_part = lax.dot_general(
        up_matrix, rows_x, (((0,), (1,)), ((), ())), preferred_element_type=jnp.float32
    )
    down_part = lax.dot_general(
        down_matrix, rows_dy, (((1,), (1,)), ((), ())), preferred_element_type=jnp.float32
    )
    summed = lax.psum_scatter(
        jnp.stack([up_part, down_part], axis=1).astype(jnp.bfloat16),
        "section",
        scatter_dimension=0,
        tiled=True,
    ).astype(jnp.float32)
    pre = summed[:, 0, :]
    dhid = summed[:, 1, :]
    hidden = jax.nn.silu(pre).astype(jnp.bfloat16)
    sigma = jax.nn.sigmoid(pre)
    dpre = (dhid * sigma * (1.0 + pre * (1.0 - sigma))).astype(jnp.bfloat16)
    hidden_piece = lax.all_gather(hidden, "section", axis=0, tiled=True)
    dpre_piece = lax.all_gather(dpre, "section", axis=0, tiled=True)
    out_y = lax.dot_general(
        hidden_piece, down_matrix, (((0,), (0,)), ((), ())), preferred_element_type=jnp.float32
    )
    out_dx = lax.dot_general(
        dpre_piece, up_matrix, (((0,), (1,)), ((), ())), preferred_element_type=jnp.float32
    )
    out_y, out_dx = (out_y, out_dx)
    return (out_y.astype(jnp.bfloat16), out_dx.astype(jnp.bfloat16))


def local(tokens, grad_out, expert_ids, route_weight, up_weight, down_weight):
    tok_count, features = tokens.shape
    top_k = expert_ids.shape[1]
    experts = lax.axis_size("expert")
    capacity = CAP
    route_count = tok_count * top_k
    chosen = expert_ids.reshape(route_count)
    onehot = (chosen[:, None] == jnp.arange(experts, dtype=jnp.int32)[None, :]).astype(jnp.int32)
    before = jnp.sum((jnp.cumsum(onehot, axis=0) - onehot) * onehot, axis=1)
    slot_count = experts * capacity
    slot = jnp.where(chosen < experts, chosen * capacity + before, slot_count)
    table = jnp.full((slot_count + 1,), route_count, jnp.int32)
    table = table.at[slot].set(jnp.arange(route_count, dtype=jnp.int32))[:slot_count]
    token_of = table // top_k
    zero_row = jnp.zeros((1, features), jnp.bfloat16)
    tok_padded = jnp.concatenate([tokens, zero_row], axis=0)
    grad_padded = jnp.concatenate([grad_out, zero_row], axis=0)
    gate_padded = jnp.concatenate(
        [route_weight.reshape(route_count), jnp.zeros((1,), jnp.float32)], axis=0
    )
    send_x = tok_padded[token_of].reshape(experts, capacity, features)
    send_dy = (gate_padded[table][:, None] * grad_padded[token_of].astype(jnp.float32)).astype(
        jnp.bfloat16
    )
    send_dy = send_dy.reshape(experts, capacity, features)
    up_matrix = up_weight[0]
    down_matrix = down_weight[0]
    recv_x, recv_dy = (
        lax.all_to_all(send_x, "expert", split_axis=0, concat_axis=0, tiled=True),
        lax.all_to_all(send_dy, "expert", split_axis=0, concat_axis=0, tiled=True),
    )
    out_y, out_dx = expert_rows(
        recv_x.reshape(slot_count, features),
        recv_dy.reshape(slot_count, features),
        up_matrix,
        down_matrix,
    )
    back_y, back_dx = (
        lax.all_to_all(
            out_y.reshape(experts, capacity, features),
            "expert",
            split_axis=0,
            concat_axis=0,
            tiled=True,
        ),
        lax.all_to_all(
            out_dx.reshape(experts, capacity, features),
            "expert",
            split_axis=0,
            concat_axis=0,
            tiled=True,
        ),
    )
    y_padded = jnp.concatenate([back_y.reshape(slot_count, features), zero_row], axis=0)
    dx_padded = jnp.concatenate([back_dx.reshape(slot_count, features), zero_row], axis=0)
    picked_y = y_padded[slot].reshape(tok_count, top_k, features).astype(jnp.float32)
    picked_dx = dx_padded[slot].reshape(tok_count, top_k, features).astype(jnp.float32)
    mixed = jnp.sum(picked_y * route_weight[:, :, None], axis=1).astype(jnp.bfloat16)
    grad_tokens = jnp.sum(picked_dx, axis=1).astype(jnp.bfloat16)
    return (mixed, grad_tokens)


def solution(mesh):
    return jax.shard_map(
        local,
        mesh=mesh,
        in_specs=(
            P("expert", "section"),
            P("expert", "section"),
            P("expert", None),
            P("expert", None),
            P("expert", "section", None),
            P("expert", None, "section"),
        ),
        out_specs=(P("expert", "section"), P("expert", "section")),
        check_vma=False,
    )
```

profile of v0, /device:TPU:1, one launch (start us, length us, event | category | flops | bytes accessed | tf_op | source)
XLA Modules:
  0.0 372.9 jit_solution(5375337180703101667)
XLA Ops:
  11.3 9.1 %reduce-window.6 = s32[32,16,128]{2,1,0:T(8,128)S(1)} reduce-window(s32[32,16,128]{2,1,0:T(8,128)S(1)} %fusion.18, s32[]{:T(128)} %constant.15.clone.1), window={size=1x1x128 pad=0_0x0_0x127_0}, to_apply=%region_0.0 | reduce-window | flops 8323072 | bytes 524292 | tf_op jit(solution)/shard_map/reduce-window
  21.2 8.0 %scatter_custom_fusion = s32[385]{0:T(512)S(1)} fusion(s32[2048]{0:T(1024)S(1)} %bitcast.77, s32[2048]{0:T(1024)S(1)} %iota.11, s32[]{:T(128)} %constant.17.clone.1), kind=kCustom, calls=%fused_computation.54 | custom fusion | bytes 1544 | tf_op jit(solution)/shard_map/scatter | solution.py:51
  29.3 2.5 gather_fusion.1
  32.2 2.1 gather_fusion.2
  35.3 18.7 %all-to-all-start.1 = ((bf16[32,12,448]{2,1,0:T(8,128)(2,1)}), bf16[32,12,448]{2,1,0:T(8,128)(2,1)S(1)}, u32[]{:S(2)}, u32[]{:S(2)}) async-start(bf16[32,12,448]{2,1,0:T(8,128)(2,1)} %multiply_convert_fusion), calls=%async_computation.1 | async-start | bytes 1048576 | tf_op jit(solution)/shard_map/all_to_all | solution.py:68
  54.1 2.1 gather_fusion
  57.1 29.0 %all-to-all-done.1 = bf16[32,12,448]{2,1,0:T(8,128)(2,1)S(1)} async-done(((bf16[32,12,448]{2,1,0:T(8,128)(2,1)}), bf16[32,12,448]{2,1,0:T(8,128)(2,1)S(1)}, u32[]{:S(2)}, u32[]{:S(2)}) %all-to-all-start.1) | async-done | bytes 344096 | tf_op jit(solution)/shard_map/all_to_all | solution.py:68
  86.1 5.8 %all-to-all-start = ((bf16[32,12,448]{2,1,0:T(8,128)(2,1)}), bf16[32,12,448]{2,1,0:T(8,128)(2,1)S(1)}, u32[]{:S(2)}, u32[]{:S(2)}) async-start(bf16[32,12,448]{2,1,0:T(8,128)(2,1)} %reshape.106), calls=%async_computation | async-start | bytes 1048576 | tf_op jit(solution)/shard_map/all_to_all | solution.py:67
  92.2 3.6 fusion.2
  95.8 28.3 %all-to-all-done = bf16[32,12,448]{2,1,0:T(8,128)(2,1)S(1)} async-done(((bf16[32,12,448]{2,1,0:T(8,128)(2,1)}), bf16[32,12,448]{2,1,0:T(8,128)(2,1)S(1)}, u32[]{:S(2)}, u32[]{:S(2)}) %all-to-all-start) | async-done | bytes 344096 | tf_op jit(solution)/shard_map/all_to_all | solution.py:67
  125.8 1.9 pad_maximum_fusion
  127.7 4.6 %copy.42 = bf16[2048,768]{1,0:T(8,128)(2,1)} copy(bf16[2048,768]{0,1:T(8,128)(2,1)} %bitcast.71) | data formatting | bytes 6291456
  132.4 62.6 %reduce-scatter.4.cloned.1.call-done = bf16[128,768]{1,0:T(8,128)(2,1)} async-done(((bf16[2048,768]{1,0:T(8,128)(2,1)}), bf16[128,768]{1,0:T(8,128)(2,1)}) %reduce-scatter.4.cloned.1.call-update) | async-done | bytes 196624
  197.7 44.8 %all-gather.5.cloned.1.call-done = bf16[2048,384]{0,1:T(8,128)(2,1)} async-done(((bf16[128,384]{0,1:T(8,128)(2,1)}), bf16[2048,384]{0,1:T(8,128)(2,1)}) %all-gather.5.cloned.1.call-update) | async-done | bytes 1572880 | tf_op jit(solution)/shard_map/all_gather | solution.py:28
  242.5 2.5 fusion.9
  246.1 14.5 %all-to-all-start.3 = ((bf16[32,12,448]{2,1,0:T(8,128)(2,1)}), bf16[32,12,448]{2,1,0:T(8,128)(2,1)S(1)}, u32[]{:S(2)}, u32[]{:S(2)}) async-start(bf16[32,12,448]{2,1,0:T(8,128)(2,1)} %reshape.112), calls=%async_computation.3 | async-start | bytes 1048576 | tf_op jit(solution)/shard_map/all_to_all | solution.py:84
  260.6 28.4 %all-gather.3.cloned.1.call-done = bf16[2048,384]{0,1:T(8,128)(2,1)} async-done(((bf16[128,384]{0,1:T(8,128)(2,1)}), bf16[2048,384]{0,1:T(8,128)(2,1)}) %all-gather.3.cloned.1.call-update) | async-done | bytes 1572880 | tf_op jit(solution)/shard_map/all_gather | solution.py:27
  289.0 3.1 fusion.12
  293.2 14.7 %all-to-all-start.2 = ((bf16[32,12,448]{2,1,0:T(8,128)(2,1)}), bf16[32,12,448]{2,1,0:T(8,128)(2,1)S(1)}, u32[]{:S(2)}, u32[]{:S(2)}) async-start(bf16[32,12,448]{2,1,0:T(8,128)(2,1)} %reshape.110), calls=%async_computation.2 | async-start | bytes 1048576 | tf_op jit(solution)/shard_map/all_to_all | solution.py:77
  308.2 32.0 %all-to-all-done.2 = bf16[32,12,448]{2,1,0:T(8,128)(2,1)S(1)} async-done(((bf16[32,12,448]{2,1,0:T(8,128)(2,1)}), bf16[32,12,448]{2,1,0:T(8,128)(2,1)S(1)}, u32[]{:S(2)}, u32[]{:S(2)}) %all-to-all-start.2) | async-done | bytes 344096 | tf_op jit(solution)/shard_map/all_to_all | solution.py:77
  340.4 9.2 %gather_fusion.3 = bf16[2048,448]{1,0:T(8,128)(2,1)} fusion(bf16[385,448]{1,0:T(8,128)(2,1)S(1)} %concatenate.18, s32[2048]{0:T(1024)S(1)} %broadcast_clamp_fusion), kind=kCustom, calls=%fused_computation.3 | custom fusion | bytes 3678208 | tf_op jit(solution)/shard_map/gather | solution.py:94
  349.6 3.0 fusion
  353.4 9.2 %gather_fusion.4 = bf16[2048,448]{1,0:T(8,128)(2,1)} fusion(bf16[385,448]{1,0:T(8,128)(2,1)S(1)} %concatenate.19, s32[2048]{0:T(1024)S(1)} %broadcast_clamp_fusion), kind=kCustom, calls=%fused_computation.4 | custom fusion | bytes 3678208 | tf_op jit(solution)/shard_map/gather | solution.py:95
  362.6 3.0 bitcast_reduce_fusion
  (62 shorter events, 16.0 us)
Async XLA Ops:
  7.2 117.2 %copy-start = (bf16[1,448,2048]{2,1,0:T(8,128)(2,1)S(1)}, bf16[1,448,2048]{2,1,0:T(8,128)(2,1)}, u32[]{:S(2)}) copy-start(bf16[1,448,2048]{2,1,0:T(8,128)(2,1)} %param.10) | copy-start | bytes 5505028
  20.4 11.6 %copy-start.2 = (bf16[256,448]{0,1:T(8,128)(2,1)S(1)}, bf16[256,448]{0,1:T(8,128)(2,1)}, u32[]{:S(2)}) copy-start(bf16[256,448]{0,1:T(8,128)(2,1)} %param.7) | copy-start | bytes 688132
  34.3 19.6 %copy-start.3 = (bf16[256,448]{0,1:T(8,128)(2,1)S(1)}, bf16[256,448]{0,1:T(8,128)(2,1)}, u32[]{:S(2)}) copy-start(bf16[256,448]{0,1:T(8,128)(2,1)} %param.6) | copy-start | bytes 688132
  35.3 50.8 %all-to-all-start.1 = ((bf16[32,12,448]{2,1,0:T(8,128)(2,1)}), bf16[32,12,448]{2,1,0:T(8,128)(2,1)S(1)}, u32[]{:S(2)}, u32[]{:S(2)}) async-start(bf16[32,12,448]{2,1,0:T(8,128)(2,1)} %multiply_convert_fusion), calls=%async_computation.1 | async-start | bytes 1048576 | tf_op jit(solution)/shard_map/all_to_all | solution.py:68
  86.1 38.0 %all-to-all-start = ((bf16[32,12,448]{2,1,0:T(8,128)(2,1)}), bf16[32,12,448]{2,1,0:T(8,128)(2,1)S(1)}, u32[]{:S(2)}, u32[]{:S(2)}) async-start(bf16[32,12,448]{2,1,0:T(8,128)(2,1)} %reshape.106), calls=%async_computation | async-start | bytes 1048576 | tf_op jit(solution)/shard_map/all_to_all | solution.py:67
  92.0 103.1 %reduce-scatter.4.cloned.1.call-start = ((), (), s32[]{:S(2)}) async-start(), calls=%async_computation.7 | async-start | bytes 3342336
  124.3 1.4 copy-start.1
  132.4 110.1 %all-gather.5.cloned.1.call-start = ((), (), s32[]{:S(2)}) async-start(), calls=%async_computation.6 | async-start | bytes 1671168 | tf_op jit(solution)/shard_map/all_gather | solution.py:28
  196.9 92.1 %all-gather.3.cloned.1.call-start = ((), (), s32[]{:S(2)}) async-start(), calls=%async_computation.5 | async-start | bytes 1671168 | tf_op jit(solution)/shard_map/all_gather | solution.py:27
  246.1 47.1 %all-to-all-start.3 = ((bf16[32,12,448]{2,1,0:T(8,128)(2,1)}), bf16[32,12,448]{2,1,0:T(8,128)(2,1)S(1)}, u32[]{:S(2)}, u32[]{:S(2)}) async-start(bf16[32,12,448]{2,1,0:T(8,128)(2,1)} %reshape.112), calls=%async_computation.3 | async-start | bytes 1048576 | tf_op jit(solution)/shard_map/all_to_all | solution.py:84
  293.2 46.9 %all-to-all-start.2 = ((bf16[32,12,448]{2,1,0:T(8,128)(2,1)}), bf16[32,12,448]{2,1,0:T(8,128)(2,1)S(1)}, u32[]{:S(2)}, u32[]{:S(2)}) async-start(bf16[32,12,448]{2,1,0:T(8,128)(2,1)} %reshape.110), calls=%async_computation.2 | async-start | bytes 1048576 | tf_op jit(solution)/shard_map/all_to_all | solution.py:77
Sparse Core Ops, SparseCore 0:
  132.5 62.4 reduce-scatter.3
  197.6 44.7 all-gather.4
  245.1 43.8 all-gather.2
where the time goes:
time: 375 us; the launch traced here: 373 us
  waiting for transfers between devices  226 us (60%)
  starting transfers between devices  53.8 us (14%)
  local copies, waits for them, and re-layouts  48.2 us (13%)
  other arithmetic  20.8 us (6%)
  between operations  14.1 us (4%)
  matrix products  10.3 us (3%)
    unnamed x4, waiting for transfers between devices  63.3 us
    all_gather x1, waiting for transfers between devices, expert_rows(): dpre_piece = lax.all_gather(dpre, 'section', axis=0, tiled=True)  44.8 us
    all_to_all x1, waiting for transfers between devices, local(): lax.all_to_all(out_y.reshape(experts, capacity, features), 'expert', spli...  32 us
    all_to_all x1, waiting for transfers between devices, local(): lax.all_to_all(send_dy, 'expert', split_axis=0, concat_axis=0, tiled=True)  29 us
    all_gather x1, waiting for transfers between devices, expert_rows(): hidden_piece = lax.all_gather(hidden, 'section', axis=0, tiled=True)  28.4 us
    all_to_all x1, waiting for transfers between devices, local(): lax.all_to_all(send_x, 'expert', split_axis=0, concat_axis=0, tiled=True)  28.3 us
    all_to_all x1, starting transfers between devices, local(): lax.all_to_all(send_dy, 'expert', split_axis=0, concat_axis=0, tiled=True)  18.7 us
    all_to_all x1, starting transfers between devices, local(): lax.all_to_all(out_y.reshape(experts, capacity, features), 'expert', spli...  14.7 us
  transfers between devices with their start and end apart: 7, of which 6 were waited for; matrix products, arithmetic and copies ran while one was open for 4% of the time, Pallas kernels for 0%

commit v1 on v0

v1 whole, which is shorter than its diff:
```python
import jax
import jax.numpy as jnp
from jax import lax
from jax.experimental import pallas as pl
from jax.experimental.pallas import tpu as pltpu
from jax.sharding import PartitionSpec as P

CAP = 12
HALF = CAP // 2
TILES = 11
SHIFTS = ((0, 0, 0), (-6, 0, 1), (2, 1, 1), (-4, 1, 2), (4, 2, 2), (-2, 2, 3))
F32 = jnp.float32
BF16 = jnp.bfloat16


def pairs_of(first_tile, first_group):
    return [
        (first_tile + 3 * n, first_group + 4 * n)
        for n in range(4)
        if first_tile + 3 * n < TILES and first_group + 4 * n < 14
    ]


def dot(a, b, contract):
    return lax.dot_general(a, b, ((contract[0], contract[1]), ((), ())), preferred_element_type=F32)


def placed(rank3, shift):
    experts, _, tokens = rank3.shape
    row = lax.broadcasted_iota(jnp.int32, rank3.shape, 1).astype(F32) + float(shift)
    return jnp.where(rank3 == row, 1.0, 0.0).reshape(experts * 8, tokens)


def route(ids, gates, core, experts):
    tokens = ids.shape[1]
    expert_row = lax.broadcasted_iota(jnp.int32, (experts, tokens), 0)
    named = jnp.zeros((experts, tokens), F32)
    gate = jnp.zeros((experts, tokens), F32)
    for k in range(ids.shape[0]):
        hit = ids[k : k + 1, :] == expert_row
        named = named + jnp.where(hit, 1.0, 0.0)
        gate = gate + jnp.where(hit, gates[k : k + 1, :], 0.0)
    earlier = lax.broadcasted_iota(jnp.int32, (tokens, tokens), 0) < lax.broadcasted_iota(
        jnp.int32, (tokens, tokens), 1
    )
    before = dot(named.astype(BF16), jnp.where(earlier, 1.0, 0.0).astype(BF16), ((1,), (0,)))
    rank = before - core * float(HALF)
    kept = (named > 0.5) & (rank > -0.5) & (rank < HALF - 0.5)
    return jnp.where(kept, rank, -100.0), gate


def pack_rows(rank, gate, source):
    experts, tokens = rank.shape
    rank3 = jnp.broadcast_to(rank[:, None, :], (experts, 8, tokens))
    gate2 = jnp.broadcast_to(gate[:, None, :], (experts, 8, tokens)).reshape(experts * 8, tokens)
    tiles = [None] * TILES
    for shift, tile, group in SHIFTS:
        pairs = pairs_of(tile, group)
        onehot = placed(rank3, shift)
        weight = jnp.sum(onehot * gate2, axis=1, keepdims=True)
        stacked = jnp.concatenate([source[g] for _, g in pairs], axis=0)
        rows = dot(onehot.astype(BF16), stacked, ((1,), (1,)))
        for n, (k, g) in enumerate(pairs):
            part = rows[:, n * 128 : (n + 1) * 128]
            part = part if g < 7 else part * weight
            tiles[k] = part if tiles[k] is None else tiles[k] + part
    return jnp.concatenate([t.reshape(experts, 8, 128) for t in tiles], axis=1)


def split_tiles(message):
    blocks = message.shape[0]
    wide = message.astype(F32).reshape(blocks, TILES, 8, 128)
    return [wide[:, k].reshape(blocks * 8, 128).astype(BF16) for k in range(TILES)]


def chosen_rows(blocks, shift, flipped):
    shape = (blocks * 8, blocks * HALF) if flipped else (blocks * HALF, blocks * 8)
    compact = lax.broadcasted_iota(jnp.int32, shape, 1 if flipped else 0)
    packed = lax.broadcasted_iota(jnp.int32, shape, 0 if flipped else 1)
    bits = blocks.bit_length() - 1
    same = (packed >> 3 == (compact & (blocks - 1))) & ((packed & 7) + shift == compact >> bits)
    return jnp.where(same, 1.0, 0.0).astype(BF16)


def unpack_rows(tiles, blocks):
    groups = [None] * 14
    for shift, tile, group in SHIFTS:
        pairs = pairs_of(tile, group)
        stacked = jnp.concatenate([tiles[k] for k, _ in pairs], axis=1)
        rows = dot(chosen_rows(blocks, shift, False), stacked, ((1,), (0,)))
        for n, (k, g) in enumerate(pairs):
            part = rows[:, n * 128 : (n + 1) * 128]
            groups[g] = part if groups[g] is None else groups[g] + part
    return groups


def repack_rows(groups, blocks):
    tiles = [None] * TILES
    for shift, tile, group in SHIFTS:
        pairs = pairs_of(tile, group)
        stacked = jnp.concatenate([groups[g] for _, g in pairs], axis=1)
        rows = dot(chosen_rows(blocks, shift, True), stacked, ((1,), (0,)))
        for n, (k, g) in enumerate(pairs):
            part = rows[:, n * 128 : (n + 1) * 128]
            tiles[k] = part if tiles[k] is None else tiles[k] + part
    return jnp.concatenate([t.reshape(blocks, 8, 128) for t in tiles], axis=1)


def combine_rows(rank, gate, tiles):
    experts, tokens = rank.shape
    rank3 = jnp.broadcast_to(rank[:, None, :], (experts, 8, tokens))
    gate2 = jnp.broadcast_to(gate[:, None, :], (experts, 8, tokens)).reshape(experts * 8, tokens)
    groups = [None] * 14

    def add(g, part):
        groups[g] = part if groups[g] is None else groups[g] + part

    for shift, tile, group in SHIFTS:
        pairs = pairs_of(tile, group)
        onehot = placed(rank3, shift)
        weight = onehot * gate2
        high = weight.astype(BF16)
        low = (weight - high.astype(F32)).astype(BF16)
        for scaled in (True, False):
            some = [(k, g) for k, g in pairs if (g < 7) == scaled]
            stacked = jnp.concatenate([tiles[k] for k, _ in some], axis=1)
            if scaled:
                sums = dot(stacked, high, ((0,), (0,))) + dot(stacked, low, ((0,), (0,)))
            else:
                sums = dot(stacked, onehot.astype(BF16), ((0,), (0,)))
            for n, (_, g) in enumerate(some):
                add(g, sums[n * 128 : (n + 1) * 128])
    return jnp.concatenate(groups[:7], axis=0), jnp.concatenate(groups[7:], axis=0)


def send_kernel(core_ref, ids_ref, gates_ref, tok_a, tok_b, dy_a, dy_b, out_ref, rank_ref, gate_ref):
    experts = out_ref.shape[0]
    rank, gate = route(ids_ref[...], gates_ref[...], core_ref[0, 0].astype(F32), experts)
    rank_ref[...] = rank
    gate_ref[...] = gate
    feats = jnp.concatenate([tok_a[...], tok_b[...], dy_a[...], dy_b[...]], axis=0)
    source = [feats[g * 128 : (g + 1) * 128] for g in range(14)]
    out_ref[...] = pack_rows(rank, gate, source).astype(BF16)


def up_kernel(recv_ref, up_a, up_b, down_a, down_b, out_ref, x_ref, dy_ref):
    @pl.when(pl.program_id(0) == 0)
    def _():
        blocks = recv_ref.shape[0]
        groups = unpack_rows(split_tiles(recv_ref[...]), blocks)
        for g in range(7):
            x_ref[:, g * 128 : (g + 1) * 128] = groups[g].astype(BF16)
            dy_ref[:, g * 128 : (g + 1) * 128] = groups[7 + g].astype(BF16)

    rows = x_ref.shape[0]
    up = jnp.concatenate([up_a[...], up_b[...]], axis=0)
    down = jnp.concatenate([down_a[...], down_b[...]], axis=0)
    out_ref[0, :rows, :] = dot(x_ref[...], up, ((1,), (0,))).astype(BF16)
    out_ref[0, rows:, :] = dot(dy_ref[...], down, ((1,), (0,))).astype(BF16)


def act_kernel(parts_ref, out_ref):
    summed = jnp.sum(parts_ref[...].astype(F32), axis=0)
    pre = summed[0]
    dhid = summed[1]
    sigma = 1.0 / (1.0 + jnp.exp(-pre))
    hidden = (pre * sigma).astype(BF16)
    dpre = (dhid * sigma * (1.0 + pre * (1.0 - sigma))).astype(BF16)
    for q in range(out_ref.shape[0]):
        out_ref[q, 0] = hidden
        out_ref[q, 1] = dpre


def down_kernel(recv_ref, up_a, up_b, down_a, down_b, out_ref, y_ref, dx_ref):
    step = pl.program_id(0)
    rows = y_ref.shape[0]
    up = jnp.concatenate([up_a[...], up_b[...]], axis=0)
    down = jnp.concatenate([down_a[...], down_b[...]], axis=0)
    y = dot(recv_ref[0, :rows, :], down, ((1,), (1,)))
    dx = dot(recv_ref[0, rows:, :], up, ((1,), (1,)))

    @pl.when(step == 0)
    def _():
        y_ref[...] = y
        dx_ref[...] = dx

    @pl.when(step > 0)
    def _():
        y_ref[...] += y
        dx_ref[...] += dx

    @pl.when(step == pl.num_programs(0) - 1)
    def _():
        blocks = out_ref.shape[0]
        groups = [ref[:, g * 128 : (g + 1) * 128].astype(BF16) for ref in (y_ref, dx_ref) for g in range(7)]
        out_ref[...] = repack_rows(groups, blocks).astype(BF16)


def combine_kernel(rank_ref, gate_ref, recv_ref, mixed_ref, grad_ref, other_ref):
    mixed, grad = combine_rows(rank_ref[...], gate_ref[...], split_tiles(recv_ref[...]))
    width = mixed_ref.shape[0]
    mixed_ref[...] = mixed[:width]
    grad_ref[...] = grad[:width]
    other_ref[0] = mixed[width:].astype(BF16)
    other_ref[1] = grad[width:].astype(BF16)


def params():
    return pltpu.CompilerParams(vmem_limit_bytes=40 * 1024 * 1024)


def whole(shape):
    return pl.BlockSpec(shape, lambda *_: (0,) * len(shape))


def local(tokens, grad_out, expert_ids, route_weight, up_weight, down_weight):
    tok_count, features = tokens.shape
    experts = lax.axis_size("expert")
    sections = lax.axis_size("section")
    chips = sections // 2
    hidden_units = up_weight.shape[2]
    block = hidden_units // chips
    rows = experts * HALF
    swap = [(s, s ^ 1) for s in range(sections)]
    same_core = [[2 * q + c for q in range(chips)] for c in range(2)]
    core = (lax.axis_index("section") & 1).astype(jnp.int32).reshape(1, 1)

    tok_a, dy_a = tokens.T, grad_out.T
    tok_b, dy_b = lax.ppermute(tok_a, "section", swap), lax.ppermute(dy_a, "section", swap)
    message = jax.ShapeDtypeStruct((experts, 8 * TILES, 128), BF16)
    by_expert = jax.ShapeDtypeStruct((experts, tok_count), F32)
    send, rank, gate = pl.pallas_call(
        send_kernel,
        out_shape=(message, by_expert, by_expert),
        in_specs=[pl.BlockSpec(memory_space=pltpu.SMEM)] + [pl.BlockSpec(memory_space=pltpu.VMEM)] * 6,
        out_specs=[pl.BlockSpec(memory_space=pltpu.VMEM)] * 3,
        compiler_params=params(),
        name="send_rows",
    )(core, expert_ids.T, route_weight.T, tok_a, tok_b, dy_a, dy_b)
    recv = lax.all_to_all(send, "expert", split_axis=0, concat_axis=0, tiled=True)

    up_a, down_a = up_weight[0], down_weight[0].T
    up_b, down_b = lax.ppermute(up_a, "section", swap), lax.ppermute(down_a, "section", swap)
    weights = (up_a, up_b, down_a, down_b)
    weight_specs = [pl.BlockSpec((features, block), lambda q: (0, q))] * 4
    parts = pl.pallas_call(
        up_kernel,
        grid=(chips,),
        out_shape=jax.ShapeDtypeStruct((chips, 2 * rows, block), BF16),
        in_specs=[whole(message.shape)] + weight_specs,
        out_specs=pl.BlockSpec((1, 2 * rows, block), lambda q: (q, 0, 0)),
        scratch_shapes=[pltpu.VMEM((rows, 2 * features), BF16)] * 2,
        compiler_params=params(),
        name="up_products",
    )(recv, *weights)
    parts = lax.all_to_all(
        parts, "section", split_axis=0, concat_axis=0, axis_index_groups=same_core, tiled=True
    )
    steps = 4
    act_spec = pl.BlockSpec((chips, 2, rows // steps, block), lambda i: (0, 0, i, 0))
    acts = pl.pallas_call(
        act_kernel,
        grid=(steps,),
        out_shape=jax.ShapeDtypeStruct((chips, 2, rows, block), BF16),
        in_specs=[act_spec],
        out_specs=act_spec,
        compiler_params=params(),
        name="activations",
    )(parts.reshape(chips, 2, rows, block))
    acts = lax.all_to_all(
        acts.reshape(chips, 2 * rows, block),
        "section",
        split_axis=0,
        concat_axis=0,
        axis_index_groups=same_core,
        tiled=True,
    )
    back = pl.pallas_call(
        down_kernel,
        grid=(chips,),
        out_shape=message,
        in_specs=[pl.BlockSpec((1, 2 * rows, block), lambda q: (q, 0, 0))] + weight_specs,
        out_specs=whole(message.shape),
        scratch_shapes=[pltpu.VMEM((rows, 2 * features), F32)] * 2,
        compiler_params=params(),
        name="down_products",
    )(acts, *weights)
    back = lax.all_to_all(back, "expert", split_axis=0, concat_axis=0, tiled=True)
    own = jax.ShapeDtypeStruct((features, tok_count), F32)
    mixed, grad, other = pl.pallas_call(
        combine_kernel,
        out_shape=(own, own, jax.ShapeDtypeStruct((2, features, tok_count), BF16)),
        in_specs=[pl.BlockSpec(memory_space=pltpu.VMEM)] * 3,
        out_specs=[pl.BlockSpec(memory_space=pltpu.VMEM)] * 3,
        compiler_params=params(),
        name="combine_rows",
    )(rank, gate, back)
    other = lax.ppermute(other, "section", swap).astype(F32)
    return (mixed + other[0]).astype(BF16).T, (grad + other[1]).astype(BF16).T


def solution(mesh):
    return jax.shard_map(
        local,
        mesh=mesh,
        in_specs=(
            P("expert", "section"),
            P("expert", "section"),
            P("expert", None),
            P("expert", None),
            P("expert", "section", None),
            P("expert", None, "section"),
        ),
        out_specs=(P("expert", "section"), P("expert", "section")),
        check_vma=False,
    )
```

time: 375 us -> 188 us (0.50)
  waiting for transfers between devices: 226 us -> 35.6 us
  blocking collectives: 0 us -> 89.9 us
  local copies, waits for them, and re-layouts: 48.2 us -> 10.3 us
  other arithmetic: 20.8 us -> 0.92 us
  starting transfers between devices: 53.8 us -> 35.4 us
  Pallas kernels: 0 us -> 14.1 us
  between operations: 14.1 us -> 0.77 us
  matrix products: 10.3 us -> 0 us
    all_to_all x0 -> x3, blocking collectives: none -> 89.9 us  [the longest x1 44.2 us: local(): lax.all_to_all(back, 'expert', split_axis=0, concat_axis=0, tiled=True)]
    all_gather x2 -> x0, waiting for transfers between devices: 73.2 us -> none  [the longest x1 44.8 us: expert_rows(): dpre_piece = lax.all_gather(dpre, 'section', axis=0, tiled=True)]
    unnamed x4 -> x0, waiting for transfers between devices: 63.3 us -> none
    all_to_all x4 -> x1, waiting for transfers between devices: 89.3 us -> 29.6 us  [local(): lax.all_to_all(send, 'expert', split_axis=0, concat_axis=0, tiled=True)]
    all_to_all x4 -> x1, starting transfers between devices: 53.7 us -> 12.5 us  [local(): lax.all_to_all(send, 'expert', split_axis=0, concat_axis=0, tiled=True)]
    gather x5 -> x0, local copies, waits for them, and re-layouts: 25.1 us -> none  [the longest x1 9.2 us: local(): y_padded[slot].reshape(tok_count, top_k, features).astype(jnp.float32)]
    ppermute x0 -> x5, starting transfers between devices: none -> 23 us  [the longest x1 8.92 us: local(): lax.ppermute(tok_a, 'section', swap)]
    pallas_call x0 -> x5, Pallas kernels: none -> 14.1 us  [the longest x1 6.22 us: local(): pl.pallas_call(down_kernel, grid=(chips,), out_shape=message, in_specs=[p...]
  transfers between devices with their start and end apart: 7 -> 6, of which waited for: 6 -> 5; matrix products, arithmetic and copies ran while one was open for 4% -> 0% of each run, Pallas kernels for 0% -> 0%
where the time goes in v1:
time: 188 us; the launch traced here: 187 us
  blocking collectives  89.9 us (48%)
  waiting for transfers between devices  35.6 us (19%)
  starting transfers between devices  35.4 us (19%)
  Pallas kernels  14.1 us (8%)
  local copies, waits for them, and re-layouts  10.3 us (5%)
    all_to_all x1, blocking collectives, local(): lax.all_to_all(back, 'expert', split_axis=0, concat_axis=0, tiled=True)  44.2 us
    all_to_all x1, waiting for transfers between devices, local(): lax.all_to_all(send, 'expert', split_axis=0, concat_axis=0, tiled=True)  29.6 us
    all_to_all x1, blocking collectives, local(): lax.all_to_all(parts, 'section', split_axis=0, concat_axis=0, axis_index_...  24 us
    all_to_all x1, blocking collectives, local(): lax.all_to_all(acts.reshape(chips, 2 * rows, block), 'section', split_axi...  21.7 us
    all_to_all x1, starting transfers between devices, local(): lax.all_to_all(send, 'expert', split_axis=0, concat_axis=0, tiled=True)  12.5 us
    unnamed x24, local copies, waits for them, and re-layouts  10.3 us
    ppermute x1, starting transfers between devices, local(): lax.ppermute(tok_a, 'section', swap)  8.92 us
    ppermute x1, starting transfers between devices, local(): other = lax.ppermute(other, 'section', swap).astype(F32)  7.81 us
  transfers between devices with their start and end apart: 6, of which 5 were waited for; matrix products, arithmetic and copies ran while one was open for 0% of the time, Pallas kernels for 0%

profile of v1, /device:TPU:1, one launch (start us, length us, event | category | flops | bytes accessed | tf_op | source)
XLA Modules:
  0.0 186.9 jit_solution(16327623285383420515)
XLA Ops:
  0.6 8.9 %collective-permute-start = (bf16[448,256]{1,0:T(8,128)(2,1)}, bf16[448,256]{1,0:T(8,128)(2,1)S(1)}, u32[]{:S(2)}, u32[]{:S(2)}) collective-permute-start(bf16[448,256]{1,0:T(8,128)(2,1)} %bitcast.39), channel_id=1, source_target_pairs={{0,32},{32,0},{64,96},{96,64},{128,160},{160,128},{192,224},{224,1... | collective-permute-start | bytes 688136 | tf_op jit(solution)/shard_map/ppermute | solution.py:229
  9.6 1.9 %collective-permute-start.1 = (bf16[448,256]{1,0:T(8,128)(2,1)}, bf16[448,256]{1,0:T(8,128)(2,1)S(1)}, u32[]{:S(2)}, u32[]{:S(2)}) collective-permute-start(bf16[448,256]{1,0:T(8,128)(2,1)} %bitcast.41), channel_id=1, source_target_pairs={{0,32},{32,0},{64,96},{96,64},{128,160},{160,128},{192,224},{224,1... | collective-permute-start | bytes 688136 | tf_op jit(solution)/shard_map/ppermute | solution.py:229
  11.5 1.6 collective-permute-done.1.dy_b
  13.2 0.9 copy-done.8
  14.1 0.9 copy-done.9
  16.4 1.7 send_rows.1
  18.2 12.5 %all-to-all-start = ((bf16[32,88,128]{2,1,0:T(8,128)(2,1)}), bf16[32,88,128]{2,1,0:T(8,128)(2,1)S(1)}, u32[]{:S(2)}, u32[]{:S(2)}) async-start(bf16[32,88,128]{2,1,0:T(8,128)(2,1)} %get-tuple-element.10), calls=%async_computation | async-start | bytes 1441792 | tf_op jit(solution)/shard_map/all_to_all | solution.py:240
  30.6 2.3 %collective-permute-start.2 = (bf16[448,2048]{1,0:T(8,128)(2,1)S(1)}, bf16[448,2048]{1,0:T(8,128)(2,1)S(1)}, u32[]{:S(2)}, u32[]{:S(2)}) collective-permute-start(bf16[448,2048]{1,0:T(8,128)(2,1)S(1)} %bitcast.31), channel_id=1, source_target_pairs={{0,32},{32,0},{64,96},{96,64},{128,160},{160,128},{192,224},{224,1... | collective-permute-start | bytes 5505032 | tf_op jit(solution)/shard_map/ppermute | solution.py:243
  33.0 2.0 %collective-permute-start.3 = (bf16[448,2048]{1,0:T(8,128)(2,1)}, bf16[448,2048]{1,0:T(8,128)(2,1)S(1)}, u32[]{:S(2)}, u32[]{:S(2)}) collective-permute-start(bf16[448,2048]{1,0:T(8,128)(2,1)} %bitcast.34), channel_id=1, source_target_pairs={{0,32},{32,0},{64,96},{96,64},{128,160},{160,128},{192,224},{224,1... | collective-permute-start | bytes 5505032 | tf_op jit(solution)/shard_map/ppermute | solution.py:243
  35.0 1.4 collective-permute-done.2.up_b
  36.4 1.3 copy-done.2
  37.6 1.6 collective-permute-done.3.down_b
  39.2 1.2 copy-done.5
  40.4 29.6 %all-to-all-done.recv_ref = bf16[32,88,128]{2,1,0:T(8,128)(2,1)S(1)} async-done(((bf16[32,88,128]{2,1,0:T(8,128)(2,1)}), bf16[32,88,128]{2,1,0:T(8,128)(2,1)S(1)}, u32[]{:S(2)}, u32[]{:S(2)}) %all-to-all-start) | async-done | bytes 720928 | tf_op jit(solution)/shard_map/all_to_all | solution.py:240
  70.0 1.5 copy-done.1
  71.5 1.5 copy-done.3
  73.0 1.5 copy-done.6
  74.5 4.7 %up_products.1 = bf16[8,384,256]{2,1,0:T(8,128)(2,1)S(1)} custom-call(bf16[32,88,128]{2,1,0:T(8,128)(2,1)S(1)} %all-to-all-done.recv_ref, bf16[448,2048]{1,0:T(8,128)(2,1)S(1)} %bitcast.32, bf16[448,2048]{1,0:T(8,128)(2,1)S(1)} %copy-done.3, bf16[448,2048]{1,0:T(8,128)(2,1)S(1)} %bitcast.35, bf16[448,2048]{1,0:T(8,128)(2,1)S(1)} %copy-done.6), custom_call_target="tpu_custom_call" | custom-call | tf_op jit(solution)/shard_map/up_products/pallas_call | solution.py:246
  79.2 24.0 %all_to_all.20 = bf16[8,384,256]{2,1,0:T(8,128)(2,1)S(1)} all-to-all(bf16[8,384,256]{2,1,0:T(8,128)(2,1)S(1)} %up_products.1), channel_id=1, replica_groups={{0,64,128,192,256,320,384,448},{32,96,160,224,288,352,416,480},{1,65,12..., dimensions={0} | all-to-all | bytes 3145728 | tf_op jit(solution)/shard_map/all_to_all | solution.py:256
  103.8 21.7 %all_to_all.21.recv_ref = bf16[8,384,256]{2,1,0:T(8,128)(2,1)S(1)} all-to-all(bf16[8,384,256]{2,1,0:T(8,128)(2,1)S(1)} %bitcast.38), channel_id=1, replica_groups={{0,64,128,192,256,320,384,448},{32,96,160,224,288,352,416,480},{1,65,12..., dimensions={0} | all-to-all | bytes 3145728 | tf_op jit(solution)/shard_map/all_to_all | solution.py:270
  125.5 6.2 %down_products.1 = bf16[32,88,128]{2,1,0:T(8,128)(2,1)S(1)} custom-call(bf16[8,384,256]{2,1,0:T(8,128)(2,1)S(1)} %all_to_all.21.recv_ref, bf16[448,2048]{1,0:T(8,128)(2,1)S(1)} %bitcast.33, bf16[448,2048]{1,0:T(8,128)(2,1)S(1)} %copy-done.4, bf16[448,2048]{1,0:T(8,128)(2,1)S(1)} %bitcast.36, bf16[448,2048]{1,0:T(8,128)(2,1)S(1)} %copy-done.7), custom_call_target="tpu_custom_call" | custom-call | tf_op jit(solution)/shard_map/down_products/pallas_call | solution.py:278
  131.7 44.2 %all_to_all.22.recv_ref = bf16[32,88,128]{2,1,0:T(8,128)(2,1)S(1)} all-to-all(bf16[32,88,128]{2,1,0:T(8,128)(2,1)S(1)} %down_products.1), channel_id=1, replica_groups=mesh['section'=16,'expert'=32] {'expert'}, dimensions={0} | all-to-all | bytes 1441792 | tf_op jit(solution)/shard_map/all_to_all | solution.py:288
  176.8 7.8 %collective-permute-start.4 = (bf16[2,448,256]{2,1,0:T(8,128)(2,1)S(1)}, bf16[2,448,256]{2,1,0:T(8,128)(2,1)S(1)}, u32[]{:S(2)}, u32[]{:S(2)}) collective-permute-start(bf16[2,448,256]{2,1,0:T(8,128)(2,1)S(1)} %get-tuple-element.12), channel_id=1, source_target_pairs={{0,32},{32,0},{64,96},{96,64},{128,160},{160,128},{192,224},{224,1... | collective-permute-start | bytes 1376264 | tf_op jit(solution)/shard_map/ppermute | solution.py:298
  184.6 1.4 collective-permute-done.4
  (22 shorter events, 3.8 us)
Async XLA Ops:
  0.6 30.0 %copy-start = (bf16[1,448,2048]{2,1,0:T(8,128)(2,1)S(1)}, bf16[1,448,2048]{2,1,0:T(8,128)(2,1)}, u32[]{:S(2)}) copy-start(bf16[1,448,2048]{2,1,0:T(8,128)(2,1)} %param.10) | copy-start | bytes 5505028
  0.6 10.9 %collective-permute-start = (bf16[448,256]{1,0:T(8,128)(2,1)}, bf16[448,256]{1,0:T(8,128)(2,1)S(1)}, u32[]{:S(2)}, u32[]{:S(2)}) collective-permute-start(bf16[448,256]{1,0:T(8,128)(2,1)} %bitcast.39), channel_id=1, source_target_pairs={{0,32},{32,0},{64,96},{96,64},{128,160},{160,128},{192,224},{224,1... | collective-permute-start | bytes 688136 | tf_op jit(solution)/shard_map/ppermute | solution.py:229
  9.6 3.6 %collective-permute-start.1 = (bf16[448,256]{1,0:T(8,128)(2,1)}, bf16[448,256]{1,0:T(8,128)(2,1)S(1)}, u32[]{:S(2)}, u32[]{:S(2)}) collective-permute-start(bf16[448,256]{1,0:T(8,128)(2,1)} %bitcast.41), channel_id=1, source_target_pairs={{0,32},{32,0},{64,96},{96,64},{128,160},{160,128},{192,224},{224,1... | collective-permute-start | bytes 688136 | tf_op jit(solution)/shard_map/ppermute | solution.py:229
  13.2 0.9 copy-start.8
  14.1 0.9 copy-start.9
  15.0 0.7 copy-start.10
  15.7 0.7 copy-start.11
  18.2 51.8 %all-to-all-start = ((bf16[32,88,128]{2,1,0:T(8,128)(2,1)}), bf16[32,88,128]{2,1,0:T(8,128)(2,1)S(1)}, u32[]{:S(2)}, u32[]{:S(2)}) async-start(bf16[32,88,128]{2,1,0:T(8,128)(2,1)} %get-tuple-element.10), calls=%async_computation | async-start | bytes 1441792 | tf_op jit(solution)/shard_map/all_to_all | solution.py:240
  30.6 5.7 %collective-permute-start.2 = (bf16[448,2048]{1,0:T(8,128)(2,1)S(1)}, bf16[448,2048]{1,0:T(8,128)(2,1)S(1)}, u32[]{:S(2)}, u32[]{:S(2)}) collective-permute-start(bf16[448,2048]{1,0:T(8,128)(2,1)S(1)} %bitcast.31), channel_id=1, source_target_pairs={{0,32},{32,0},{64,96},{96,64},{128,160},{160,128},{192,224},{224,1... | collective-permute-start | bytes 5505032 | tf_op jit(solution)/shard_map/ppermute | solution.py:243
  33.0 6.2 %collective-permute-start.3 = (bf16[448,2048]{1,0:T(8,128)(2,1)}, bf16[448,2048]{1,0:T(8,128)(2,1)S(1)}, u32[]{:S(2)}, u32[]{:S(2)}) collective-permute-start(bf16[448,2048]{1,0:T(8,128)(2,1)} %bitcast.34), channel_id=1, source_target_pairs={{0,32},{32,0},{64,96},{96,64},{128,160},{160,128},{192,224},{224,1... | collective-permute-start | bytes 5505032 | tf_op jit(solution)/shard_map/ppermute | solution.py:243
  36.4 1.3 copy-start.2
  39.2 1.2 copy-start.5
  70.0 1.5 copy-start.1
  71.5 1.5 copy-start.3
  73.0 1.5 copy-start.6
  103.2 22.3 %copy-start.7 = (bf16[448,2048]{1,0:T(8,128)(2,1)S(1)}, bf16[448,2048]{1,0:T(8,128)(2,1)}, u32[]{:S(2)}) copy-start(bf16[448,2048]{1,0:T(8,128)(2,1)} %copy-done.5) | copy-start | bytes 5505028
  103.8 21.7 %copy-start.4 = (bf16[448,2048]{1,0:T(8,128)(2,1)S(1)}, bf16[448,2048]{1,0:T(8,128)(2,1)}, u32[]{:S(2)}) copy-start(bf16[448,2048]{1,0:T(8,128)(2,1)} %copy-done.2) | copy-start | bytes 5505028
  176.8 9.2 %collective-permute-start.4 = (bf16[2,448,256]{2,1,0:T(8,128)(2,1)S(1)}, bf16[2,448,256]{2,1,0:T(8,128)(2,1)S(1)}, u32[]{:S(2)}, u32[]{:S(2)}) collective-permute-start(bf16[2,448,256]{2,1,0:T(8,128)(2,1)S(1)} %get-tuple-element.12), channel_id=1, source_target_pairs={{0,32},{32,0},{64,96},{96,64},{128,160},{160,128},{192,224},{224,1... | collective-permute-start | bytes 1376264 | tf_op jit(solution)/shard_map/ppermute | solution.py:298

commit v2 on v1

--- a/solution.py
+++ b/solution.py
@@ -6,6 +6,7 @@
 from jax.sharding import PartitionSpec as P
 
 CAP = 12
+LEAD = 8
 HALF = CAP // 2
 TILES = 11
 SHIFTS = ((0, 0, 0), (-6, 0, 1), (2, 1, 1), (-4, 1, 2), (4, 2, 2), (-2, 2, 3))
@@ -133,30 +134,45 @@
     return jnp.concatenate(groups[:7], axis=0), jnp.concatenate(groups[7:], axis=0)
 
 
-def send_kernel(core_ref, ids_ref, gates_ref, tok_a, tok_b, dy_a, dy_b, out_ref, rank_ref, gate_ref):
-    experts = out_ref.shape[0]
-    rank, gate = route(ids_ref[...], gates_ref[...], core_ref[0, 0].astype(F32), experts)
-    rank_ref[...] = rank
-    gate_ref[...] = gate
-    feats = jnp.concatenate([tok_a[...], tok_b[...], dy_a[...], dy_b[...]], axis=0)
+def route_kernel(core_ref, ids_ref, gates_ref, rank_ref, gate_ref):
+    core = core_ref[0, 0].astype(F32)
+    rank_ref[...], gate_ref[...] = route(ids_ref[...], gates_ref[...], core, rank_ref.shape[0])
+
+
+def send_kernel(rank_ref, gate_ref, own_ref, other_ref, out_ref):
+    half = own_ref.shape[0] // 2
+    feats = jnp.concatenate(
+        [own_ref[:half, :], other_ref[:half, :], own_ref[half:, :], other_ref[half:, :]], axis=0
+    )
     source = [feats[g * 128 : (g + 1) * 128] for g in range(14)]
-    out_ref[...] = pack_rows(rank, gate, source).astype(BF16)
-
-
-def up_kernel(recv_ref, up_a, up_b, down_a, down_b, out_ref, x_ref, dy_ref):
-    @pl.when(pl.program_id(0) == 0)
-    def _():
-        blocks = recv_ref.shape[0]
-        groups = unpack_rows(split_tiles(recv_ref[...]), blocks)
-        for g in range(7):
-            x_ref[:, g * 128 : (g + 1) * 128] = groups[g].astype(BF16)
-            dy_ref[:, g * 128 : (g + 1) * 128] = groups[7 + g].astype(BF16)
-
+    out_ref[...] = pack_rows(rank_ref[...], gate_ref[...], source).astype(BF16)
+
+
+def up_kernel(
+    recv_ref, up_own, up_other, down_own, down_other, out_ref, up_ref, down_ref, x_ref, dy_ref, sems
+):
+    features = up_own.shape[0]
+    copies = []
+    for i, (ref, joined) in enumerate(
+        ((up_own, up_ref), (up_other, up_ref), (down_own, down_ref), (down_other, down_ref))
+    ):
+        held = joined.at[pl.ds((i % 2) * features, features), :]
+        copies.append(pltpu.make_async_copy(ref, held, sems.at[i]))
+    for copy in copies:
+        copy.start()
+    groups = unpack_rows(split_tiles(recv_ref[...]), recv_ref.shape[0])
+    for g in range(7):
+        x_ref[:, g * 128 : (g + 1) * 128] = groups[g].astype(BF16)
+        dy_ref[:, g * 128 : (g + 1) * 128] = groups[7 + g].astype(BF16)
     rows = x_ref.shape[0]
-    up = jnp.concatenate([up_a[...], up_b[...]], axis=0)
-    down = jnp.concatenate([down_a[...], down_b[...]], axis=0)
-    out_ref[0, :rows, :] = dot(x_ref[...], up, ((1,), (0,))).astype(BF16)
-    out_ref[0, rows:, :] = dot(dy_ref[...], down, ((1,), (0,))).astype(BF16)
+    block = out_ref.shape[2]
+    for n, (lhs, joined) in enumerate(((x_ref, up_ref), (dy_ref, down_ref))):
+        copies[2 * n].wait()
+        copies[2 * n + 1].wait()
+        for q in range(out_ref.shape[0]):
+            units = slice(q * block, (q + 1) * block)
+            part = dot(lhs[...], joined[:, units], ((1,), (0,)))
+            out_ref[q, n * rows : (n + 1) * rows, :] = part.astype(BF16)
 
 
 def act_kernel(parts_ref, out_ref):
@@ -171,29 +187,18 @@
         out_ref[q, 1] = dpre
 
 
-def down_kernel(recv_ref, up_a, up_b, down_a, down_b, out_ref, y_ref, dx_ref):
-    step = pl.program_id(0)
-    rows = y_ref.shape[0]
-    up = jnp.concatenate([up_a[...], up_b[...]], axis=0)
-    down = jnp.concatenate([down_a[...], down_b[...]], axis=0)
-    y = dot(recv_ref[0, :rows, :], down, ((1,), (1,)))
-    dx = dot(recv_ref[0, rows:, :], up, ((1,), (1,)))
-
-    @pl.when(step == 0)
-    def _():
-        y_ref[...] = y
-        dx_ref[...] = dx
-
-    @pl.when(step > 0)
-    def _():
-        y_ref[...] += y
-        dx_ref[...] += dx
-
-    @pl.when(step == pl.num_programs(0) - 1)
-    def _():
-        blocks = out_ref.shape[0]
-        groups = [ref[:, g * 128 : (g + 1) * 128].astype(BF16) for ref in (y_ref, dx_ref) for g in range(7)]
-        out_ref[...] = repack_rows(groups, blocks).astype(BF16)
+def down_kernel(recv_ref, up_ref, down_ref, out_ref):
+    chips, rows, _ = recv_ref.shape
+    half = rows // 2
+    features = up_ref.shape[0]
+    groups = []
+    for first, weight_ref in ((0, down_ref), (half, up_ref)):
+        acts = jnp.concatenate([recv_ref[q, first : first + half, :] for q in range(chips)], axis=1)
+        for start in range(0, features, 256):
+            stop = min(start + 256, features)
+            out = dot(acts, weight_ref[start:stop, :], ((1,), (1,))).astype(BF16)
+            groups += [out[:, n : n + 128] for n in range(0, stop - start, 128)]
+    out_ref[...] = repack_rows(groups, out_ref.shape[0]).astype(BF16)
 
 
 def combine_kernel(rank_ref, gate_ref, recv_ref, mixed_ref, grad_ref, other_ref):
@@ -205,12 +210,19 @@
     other_ref[1] = grad[width:].astype(BF16)
 
 
-def params():
-    return pltpu.CompilerParams(vmem_limit_bytes=40 * 1024 * 1024)
-
-
-def whole(shape):
-    return pl.BlockSpec(shape, lambda *_: (0,) * len(shape))
+def in_vmem(kernel, name, outs, operands, far=(), scratch=(), mebibytes=16):
+    vmem = pl.BlockSpec(memory_space=pltpu.VMEM)
+    scalar = pl.BlockSpec(memory_space=pltpu.SMEM)
+    hbm = pl.BlockSpec(memory_space=pltpu.HBM)
+    return pl.pallas_call(
+        kernel,
+        out_shape=outs,
+        in_specs=[scalar if x.size == 1 else vmem for x in operands] + [hbm] * len(far),
+        out_specs=jax.tree.map(lambda _: vmem, outs),
+        scratch_shapes=list(scratch),
+        compiler_params=pltpu.CompilerParams(vmem_limit_bytes=mebibytes * 1024 * 1024),
+        name=name,
+    )(*operands, *far)
 
 
 def local(tokens, grad_out, expert_ids, route_weight, up_weight, down_weight):
@@ -224,38 +236,47 @@
     swap = [(s, s ^ 1) for s in range(sections)]
     same_core = [[2 * q + c for q in range(chips)] for c in range(2)]
     core = (lax.axis_index("section") & 1).astype(jnp.int32).reshape(1, 1)
-
-    tok_a, dy_a = tokens.T, grad_out.T
-    tok_b, dy_b = lax.ppermute(tok_a, "section", swap), lax.ppermute(dy_a, "section", swap)
     message = jax.ShapeDtypeStruct((experts, 8 * TILES, 128), BF16)
     by_expert = jax.ShapeDtypeStruct((experts, tok_count), F32)
-    send, rank, gate = pl.pallas_call(
-        send_kernel,
-        out_shape=(message, by_expert, by_expert),
-        in_specs=[pl.BlockSpec(memory_space=pltpu.SMEM)] + [pl.BlockSpec(memory_space=pltpu.VMEM)] * 6,
-        out_specs=[pl.BlockSpec(memory_space=pltpu.VMEM)] * 3,
-        compiler_params=params(),
-        name="send_rows",
-    )(core, expert_ids.T, route_weight.T, tok_a, tok_b, dy_a, dy_b)
-    recv = lax.all_to_all(send, "expert", split_axis=0, concat_axis=0, tiled=True)
-
-    up_a, down_a = up_weight[0], down_weight[0].T
-    up_b, down_b = lax.ppermute(up_a, "section", swap), lax.ppermute(down_a, "section", swap)
-    weights = (up_a, up_b, down_a, down_b)
-    weight_specs = [pl.BlockSpec((features, block), lambda q: (0, q))] * 4
-    parts = pl.pallas_call(
+    parts_type = jax.ShapeDtypeStruct((chips, 2 * rows, block), BF16)
+
+    def across_experts(x):
+        return lax.all_to_all(x, "expert", split_axis=0, concat_axis=0, tiled=True)
+
+    def across_chips(x):
+        return lax.all_to_all(
+            x, "section", split_axis=0, concat_axis=0, axis_index_groups=same_core, tiled=True
+        )
+
+    own = jnp.concatenate([tokens.T, grad_out.T], axis=0)
+    other = lax.ppermute(own, "section", swap)
+    rank, gate = in_vmem(
+        route_kernel, "route", (by_expert, by_expert), (core, expert_ids.T, route_weight.T)
+    )
+    up_own, down_own = up_weight[0], down_weight[0].T
+    up_other = lax.ppermute(up_own, "section", swap)
+    down_other = lax.ppermute(down_own, "section", swap)
+
+    def at_once(rows):
+        return across_experts(rows)
+
+    def in_two(rows):
+        return jnp.concatenate([across_experts(rows[:, :LEAD]), across_experts(rows[:, LEAD:])], axis=1)
+
+    send = in_vmem(send_kernel, "send_rows", message, (rank, gate, own, other))
+    recv = lax.cond(core[0, 0] == 0, at_once, in_two, send)
+
+    joined = jax.ShapeDtypeStruct((2 * features, hidden_units), BF16)
+    parts, up_both, down_both = in_vmem(
         up_kernel,
-        grid=(chips,),
-        out_shape=jax.ShapeDtypeStruct((chips, 2 * rows, block), BF16),
-        in_specs=[whole(message.shape)] + weight_specs,
-        out_specs=pl.BlockSpec((1, 2 * rows, block), lambda q: (q, 0, 0)),
-        scratch_shapes=[pltpu.VMEM((rows, 2 * features), BF16)] * 2,
-        compiler_params=params(),
-        name="up_products",
-    )(recv, *weights)
-    parts = lax.all_to_all(
-        parts, "section", split_axis=0, concat_axis=0, axis_index_groups=same_core, tiled=True
-    )
+        "up_products",
+        (parts_type, joined, joined),
+        (recv,),
+        (up_own, up_other, down_own, down_other),
+        [pltpu.VMEM((rows, 2 * features), BF16)] * 2 + [pltpu.SemaphoreType.DMA((4,))],
+        44,
+    )
+    parts = across_chips(parts)
     steps = 4
     act_spec = pl.BlockSpec((chips, 2, rows // steps, block), lambda i: (0, 0, i, 0))
     acts = pl.pallas_call(
@@ -264,39 +285,21 @@
         out_shape=jax.ShapeDtypeStruct((chips, 2, rows, block), BF16),
         in_specs=[act_spec],
         out_specs=act_spec,
-        compiler_params=params(),
+        compiler_params=pltpu.CompilerParams(vmem_limit_bytes=16 * 1024 * 1024),
         name="activations",
     )(parts.reshape(chips, 2, rows, block))
-    acts = lax.all_to_all(
-        acts.reshape(chips, 2 * rows, block),
-        "section",
-        split_axis=0,
-        concat_axis=0,
-        axis_index_groups=same_core,
-        tiled=True,
-    )
-    back = pl.pallas_call(
-        down_kernel,
-        grid=(chips,),
-        out_shape=message,
-        in_specs=[pl.BlockSpec((1, 2 * rows, block), lambda q: (q, 0, 0))] + weight_specs,
-        out_specs=whole(message.shape),
-        scratch_shapes=[pltpu.VMEM((rows, 2 * features), F32)] * 2,
-        compiler_params=params(),
-        name="down_products",
-    )(acts, *weights)
-    back = lax.all_to_all(back, "expert", split_axis=0, concat_axis=0, tiled=True)
-    own = jax.ShapeDtypeStruct((features, tok_count), F32)
-    mixed, grad, other = pl.pallas_call(
+    acts = across_chips(acts.reshape(chips, 2 * rows, block))
+    back = across_experts(in_vmem(down_kernel, "down_products", message, (acts, up_both, down_both)))
+
+    own_sum = jax.ShapeDtypeStruct((features, tok_count), F32)
+    mixed, grad, rest = in_vmem(
         combine_kernel,
-        out_shape=(own, own, jax.ShapeDtypeStruct((2, features, tok_count), BF16)),
-        in_specs=[pl.BlockSpec(memory_space=pltpu.VMEM)] * 3,
-        out_specs=[pl.BlockSpec(memory_space=pltpu.VMEM)] * 3,
-        compiler_params=params(),
-        name="combine_rows",
-    )(rank, gate, back)
-    other = lax.ppermute(other, "section", swap).astype(F32)
-    return (mixed + other[0]).astype(BF16).T, (grad + other[1]).astype(BF16).T
+        "combine_rows",
+        (own_sum, own_sum, jax.ShapeDtypeStruct((2, features, tok_count), BF16)),
+        (rank, gate, back),
+    )
+    rest = lax.ppermute(rest, "section", swap).astype(F32)
+    return (mixed + rest[0]).astype(BF16).T, (grad + rest[1]).astype(BF16).T
 
 
 def solution(mesh):

time: 188 us -> 166 us (0.88)
  waiting for transfers between devices: 35.6 us -> 19.1 us
  blocking collectives: 89.9 us -> 102 us
  starting transfers between devices: 35.4 us -> 27.5 us
  local copies, waits for them, and re-layouts: 10.3 us -> 3.58 us
  Pallas kernels: 14.1 us -> 10.9 us
    all_to_all x1, waiting for transfers between devices: 29.6 us -> 17.3 us  [across_experts(): return lax.all_to_all(x, 'expert', split_axis=0, concat_axis=0, tiled=True)]
    all_to_all x3 -> x4, blocking collectives: 89.9 us -> 102 us  [the longest x2 59.5 us: across_experts(): return lax.all_to_all(x, 'expert', split_axis=0, concat_axis=0, tiled=True)]
    ppermute x5 -> x4, starting transfers between devices: 23 us -> 15 us  [the longest x1 8.79 us: local(): up_other = lax.ppermute(up_own, 'section', swap)]
    unnamed x24 -> x12, local copies, waits for them, and re-layouts: 10.3 us -> 2.9 us
    ppermute x5 -> x4, waiting for transfers between devices: 6.04 us -> 1.79 us  [the longest x1 1.78 us: local(): rest = lax.ppermute(rest, 'section', swap).astype(F32)]
    pallas_call x4 -> x5, Pallas kernels: 13.5 us -> 10.3 us  [in_vmem(): pl.pallas_call(kernel, out_shape=outs, in_specs=[scalar if x.size == 1 el...]
  transfers between devices with their start and end apart: 6 -> 5, of which waited for: 5 -> 2; matrix products, arithmetic and copies ran while one was open for 0% -> 1% of each run, Pallas kernels for 0% -> 0%
where the time goes in v2:
time: 166 us
  blocking collectives  102 us (61%)
  starting transfers between devices  27.5 us (17%)
  waiting for transfers between devices  19.1 us (12%)
  Pallas kernels  10.9 us (7%)
  local copies, waits for them, and re-layouts  3.58 us (2%)
  other arithmetic  2.05 us (1%)
    all_to_all x2, blocking collectives, across_experts(): return lax.all_to_all(x, 'expert', split_axis=0, concat_axis=0, tiled=True)  59.5 us
    all_to_all x2, blocking collectives, across_chips(): lax.all_to_all(x, 'section', split_axis=0, concat_axis=0, axis_index_grou...  42.2 us
    all_to_all x1, waiting for transfers between devices, across_experts(): return lax.all_to_all(x, 'expert', split_axis=0, concat_axis=0, tiled=True)  17.3 us
    all_to_all x1, starting transfers between devices, across_experts(): return lax.all_to_all(x, 'expert', split_axis=0, concat_axis=0, tiled=True)  12.5 us
    pallas_call x5, Pallas kernels, in_vmem(): pl.pallas_call(kernel, out_shape=outs, in_specs=[scalar if x.size == 1 el...  10.3 us
    ppermute x1, starting transfers between devices, local(): up_other = lax.ppermute(up_own, 'section', swap)  8.79 us
  transfers between devices with their start and end apart: 5, of which 2 were waited for; matrix products, arithmetic and copies ran while one was open for 1% of the time, Pallas kernels for 0%

profile of v2, /device:TPU:1, one launch (start us, length us, event | category | flops | bytes accessed | tf_op | source)
XLA Modules:
  0.0 165.7 jit_solution(11644944793918393000)
XLA Ops:
  0.6 8.8 %collective-permute-start.1 = (bf16[448,2048]{1,0:T(8,128)(2,1)}, bf16[448,2048]{1,0:T(8,128)(2,1)}, u32[]{:S(2)}, u32[]{:S(2)}) collective-permute-start(bf16[448,2048]{1,0:T(8,128)(2,1)} %bitcast.33), channel_id=1, source_target_pairs={{0,32},{32,0},{64,96},{96,64},{128,160},{160,128},{192,224},{224,1... | collective-permute-start | bytes 5505032 | tf_op jit(solution)/shard_map/ppermute | solution.py:257
  9.4 1.9 %collective-permute-start.2 = (bf16[448,2048]{1,0:T(8,128)(2,1)}, bf16[448,2048]{1,0:T(8,128)(2,1)}, u32[]{:S(2)}, u32[]{:S(2)}) collective-permute-start(bf16[448,2048]{1,0:T(8,128)(2,1)} %bitcast.35), channel_id=1, source_target_pairs={{0,32},{32,0},{64,96},{96,64},{128,160},{160,128},{192,224},{224,1... | collective-permute-start | bytes 5505032 | tf_op jit(solution)/shard_map/ppermute | solution.py:258
  11.4 1.1 pad_maximum_fusion.1.own_ref
  12.4 2.4 %collective-permute-start = (bf16[896,256]{1,0:T(8,128)(2,1)S(1)}, bf16[896,256]{1,0:T(8,128)(2,1)S(1)}, u32[]{:S(2)}, u32[]{:S(2)}) collective-permute-start(bf16[896,256]{1,0:T(8,128)(2,1)S(1)} %pad_maximum_fusion.1.own_ref), channel_id=1, source_target_pairs={{0,32},{32,0},{64,96},{96,64},{128,160},{160,128},{192,224},{224,1... | collective-permute-start | bytes 1376264 | tf_op jit(solution)/shard_map/ppermute | solution.py:252
  14.9 0.7 copy-done.4
  15.6 0.7 copy-done.5
  16.3 0.2 route.1
  16.4 0.6 send_rows.1
  17.1 58.8 %conditional.1 = (bf16[32,88,128]{2,1,0:T(8,128)(2,1)S(1)}) conditional(s32[]{:T(128)} %convert_element_type.12, bf16[32,88,128]{2,1,0:T(8,128)(2,1)S(1)} %send_rows.1, bf16[32,88,128]{2,1,0:T(8,128)(2,1)S(1)} %send_rows.1), branch_computations={%region_0.0_spmd, %region_1.0_spmd} | conditional | flops 1441792 | bytes 4390952 | solution.py:267
  17.1 0.6 slice.8
  17.7 12.5 %all-to-all-start.1 = ((bf16[32,8,128]{2,1,0:T(8,128)(2,1)}), bf16[32,8,128]{2,1,0:T(8,128)(2,1)S(1)}, u32[]{:S(2)}, u32[]{:S(2)}) async-start(bf16[32,8,128]{2,1,0:T(8,128)(2,1)} %slice.8), calls=%async_computation.1 | async-start | bytes 131072 | tf_op jit(solution)/shard_map/cond/branch_0_fun/all_to_all | solution.py:244
  30.3 17.3 %all-to-all-done.1 = bf16[32,8,128]{2,1,0:T(8,128)(2,1)S(1)} async-done(((bf16[32,8,128]{2,1,0:T(8,128)(2,1)}), bf16[32,8,128]{2,1,0:T(8,128)(2,1)S(1)}, u32[]{:S(2)}, u32[]{:S(2)}) %all-to-all-start.1) | async-done | bytes 65568 | tf_op jit(solution)/shard_map/cond/branch_0_fun/all_to_all | solution.py:244
  47.6 28.3 %all_to_all.27 = bf16[32,80,128]{2,1,0:T(8,128)(2,1)S(1)} all-to-all(bf16[32,80,128]{2,1,0:T(8,128)(2,1)S(1)} %slice.9), channel_id=1, replica_groups=mesh['section'=16,'expert'=32] {'expert'}, dimensions={0} | all-to-all | bytes 1310720 | tf_op jit(solution)/shard_map/cond/branch_0_fun/all_to_all | solution.py:244
  76.0 1.5 copy-done.3
  77.4 5.6 %up_products.1 = (bf16[8,384,256]{2,1,0:T(8,128)(2,1)S(1)}, bf16[896,2048]{1,0:T(8,128)(2,1)}, bf16[896,2048]{1,0:T(8,128)(2,1)}) custom-call(bf16[32,88,128]{2,1,0:T(8,128)(2,1)S(1)} %get-tuple-element.25.recv_ref, bf16[448,2048]{1,0:T(8,128)(2,1)S(1)} %bitcast.34, bf16[448,2048]{1,0:T(8,128)(2,1)} %collective-permute-done.1.up_other, ...), custom_call_target="tpu_custom_call" | custom-call | tf_op jit(solution)/shard_map/up_products/pallas_call | solution.py:217
  83.1 26.0 %all_to_all.29 = bf16[8,384,256]{2,1,0:T(8,128)(2,1)S(1)} all-to-all(bf16[8,384,256]{2,1,0:T(8,128)(2,1)S(1)} %get-tuple-element.17), channel_id=1, replica_groups={{0,64,128,192,256,320,384,448},{32,96,160,224,288,352,416,480},{1,65,12..., dimensions={0} | all-to-all | bytes 3145728 | tf_op jit(solution)/shard_map/all_to_all | solution.py:247
  109.0 0.6 activations.1
  109.6 16.2 %all_to_all.30.recv_ref = bf16[8,384,256]{2,1,0:T(8,128)(2,1)S(1)} all-to-all(bf16[8,384,256]{2,1,0:T(8,128)(2,1)S(1)} %bitcast.32), channel_id=1, replica_groups={{0,64,128,192,256,320,384,448},{32,96,160,224,288,352,416,480},{1,65,12..., dimensions={0} | all-to-all | bytes 3145728 | tf_op jit(solution)/shard_map/all_to_all | solution.py:247
  125.8 3.1 %down_products.1 = bf16[32,88,128]{2,1,0:T(8,128)(2,1)S(1)} custom-call(bf16[8,384,256]{2,1,0:T(8,128)(2,1)S(1)} %all_to_all.30.recv_ref, bf16[896,2048]{1,0:T(8,128)(2,1)S(1)} %copy-done, bf16[896,2048]{1,0:T(8,128)(2,1)S(1)} %copy-done.1), custom_call_target="tpu_custom_call" | custom-call | tf_op jit(solution)/shard_map/down_products/pallas_call | solution.py:217
  128.9 31.2 %all_to_all.31.recv_ref = bf16[32,88,128]{2,1,0:T(8,128)(2,1)S(1)} all-to-all(bf16[32,88,128]{2,1,0:T(8,128)(2,1)S(1)} %down_products.1), channel_id=1, replica_groups=mesh['section'=16,'expert'=32] {'expert'}, dimensions={0} | all-to-all | bytes 1441792 | tf_op jit(solution)/shard_map/all_to_all | solution.py:244
  160.1 0.9 combine_rows.1
  161.0 1.9 %collective-permute-start.3 = (bf16[2,448,256]{2,1,0:T(8,128)(2,1)S(1)}, bf16[2,448,256]{2,1,0:T(8,128)(2,1)S(1)}, u32[]{:S(2)}, u32[]{:S(2)}) collective-permute-start(bf16[2,448,256]{2,1,0:T(8,128)(2,1)S(1)} %get-tuple-element.21), channel_id=1, source_target_pairs={{0,32},{32,0},{64,96},{96,64},{128,160},{160,128},{192,224},{224,1... | collective-permute-start | bytes 1376264 | tf_op jit(solution)/shard_map/ppermute | solution.py:301
  162.9 1.8 %collective-permute-done.3 = bf16[2,448,256]{2,1,0:T(8,128)(2,1)S(1)} collective-permute-done((bf16[2,448,256]{2,1,0:T(8,128)(2,1)S(1)}, bf16[2,448,256]{2,1,0:T(8,128)(2,1)S(1)}, u32[]{:S(2)}, u32[]{:S(2)}) %collective-permute-start.3) | collective-permute-done | bytes 458784 | tf_op jit(solution)/shard_map/ppermute | solution.py:301
  164.8 0.9 fusion.5
  (15 shorter events, 0.2 us)
Async XLA Ops:
  0.6 75.3 %collective-permute-start.1 = (bf16[448,2048]{1,0:T(8,128)(2,1)}, bf16[448,2048]{1,0:T(8,128)(2,1)}, u32[]{:S(2)}, u32[]{:S(2)}) collective-permute-start(bf16[448,2048]{1,0:T(8,128)(2,1)} %bitcast.33), channel_id=1, source_target_pairs={{0,32},{32,0},{64,96},{96,64},{128,160},{160,128},{192,224},{224,1... | collective-permute-start | bytes 5505032 | tf_op jit(solution)/shard_map/ppermute | solution.py:257
  9.4 66.5 %collective-permute-start.2 = (bf16[448,2048]{1,0:T(8,128)(2,1)}, bf16[448,2048]{1,0:T(8,128)(2,1)}, u32[]{:S(2)}, u32[]{:S(2)}) collective-permute-start(bf16[448,2048]{1,0:T(8,128)(2,1)} %bitcast.35), channel_id=1, source_target_pairs={{0,32},{32,0},{64,96},{96,64},{128,160},{160,128},{192,224},{224,1... | collective-permute-start | bytes 5505032 | tf_op jit(solution)/shard_map/ppermute | solution.py:258
  12.4 4.0 %collective-permute-start = (bf16[896,256]{1,0:T(8,128)(2,1)S(1)}, bf16[896,256]{1,0:T(8,128)(2,1)S(1)}, u32[]{:S(2)}, u32[]{:S(2)}) collective-permute-start(bf16[896,256]{1,0:T(8,128)(2,1)S(1)} %pad_maximum_fusion.1.own_ref), channel_id=1, source_target_pairs={{0,32},{32,0},{64,96},{96,64},{128,160},{160,128},{192,224},{224,1... | collective-permute-start | bytes 1376264 | tf_op jit(solution)/shard_map/ppermute | solution.py:252
  14.9 0.7 copy-start.4
  15.6 0.7 copy-start.5
  17.1 58.8 %copy-start.2 = (bf16[1,448,2048]{2,1,0:T(8,128)(2,1)S(1)}, bf16[1,448,2048]{2,1,0:T(8,128)(2,1)}, u32[]{:S(2)}) copy-start(bf16[1,448,2048]{2,1,0:T(8,128)(2,1)} %param.12) | copy-start | bytes 5505028
  17.7 29.8 %all-to-all-start.1 = ((bf16[32,8,128]{2,1,0:T(8,128)(2,1)}), bf16[32,8,128]{2,1,0:T(8,128)(2,1)S(1)}, u32[]{:S(2)}, u32[]{:S(2)}) async-start(bf16[32,8,128]{2,1,0:T(8,128)(2,1)} %slice.8), calls=%async_computation.1 | async-start | bytes 131072 | tf_op jit(solution)/shard_map/cond/branch_0_fun/all_to_all | solution.py:244
  75.9 1.5 copy-start.3
  83.0 42.8 %copy-start.1 = (bf16[896,2048]{1,0:T(8,128)(2,1)S(1)}, bf16[896,2048]{1,0:T(8,128)(2,1)}, u32[]{:S(2)}) copy-start(bf16[896,2048]{1,0:T(8,128)(2,1)} %get-tuple-element.19.down_ref) | copy-start | bytes 11010052
  109.0 16.8 %copy-start = (bf16[896,2048]{1,0:T(8,128)(2,1)S(1)}, bf16[896,2048]{1,0:T(8,128)(2,1)}, u32[]{:S(2)}) copy-start(bf16[896,2048]{1,0:T(8,128)(2,1)} %get-tuple-element.18.up_ref) | copy-start | bytes 11010052
  161.0 3.7 %collective-permute-start.3 = (bf16[2,448,256]{2,1,0:T(8,128)(2,1)S(1)}, bf16[2,448,256]{2,1,0:T(8,128)(2,1)S(1)}, u32[]{:S(2)}, u32[]{:S(2)}) collective-permute-start(bf16[2,448,256]{2,1,0:T(8,128)(2,1)S(1)} %get-tuple-element.21), channel_id=1, source_target_pairs={{0,32},{32,0},{64,96},{96,64},{128,160},{160,128},{192,224},{224,1... | collective-permute-start | bytes 1376264 | tf_op jit(solution)/shard_map/ppermute | solution.py:301

commit v3 on v2

--- a/solution.py
+++ b/solution.py
@@ -1,3 +1,5 @@
+import functools
+
 import jax
 import jax.numpy as jnp
 from jax import lax
@@ -69,9 +71,9 @@
 
 
 def split_tiles(message):
-    blocks = message.shape[0]
-    wide = message.astype(F32).reshape(blocks, TILES, 8, 128)
-    return [wide[:, k].reshape(blocks * 8, 128).astype(BF16) for k in range(TILES)]
+    blocks, rows, _ = message.shape
+    wide = message.astype(F32).reshape(blocks, rows // 8, 8, 128)
+    return [wide[:, k].reshape(blocks * 8, 128).astype(BF16) for k in range(rows // 8)]
 
 
 def chosen_rows(blocks, shift, flipped):
@@ -139,40 +141,34 @@
     rank_ref[...], gate_ref[...] = route(ids_ref[...], gates_ref[...], core, rank_ref.shape[0])
 
 
-def send_kernel(rank_ref, gate_ref, own_ref, other_ref, out_ref):
+def send_kernel(rank_ref, gate_ref, own_ref, other_ref, *out_refs):
     half = own_ref.shape[0] // 2
     feats = jnp.concatenate(
         [own_ref[:half, :], other_ref[:half, :], own_ref[half:, :], other_ref[half:, :]], axis=0
     )
     source = [feats[g * 128 : (g + 1) * 128] for g in range(14)]
-    out_ref[...] = pack_rows(rank_ref[...], gate_ref[...], source).astype(BF16)
-
-
-def up_kernel(
-    recv_ref, up_own, up_other, down_own, down_other, out_ref, up_ref, down_ref, x_ref, dy_ref, sems
-):
-    features = up_own.shape[0]
-    copies = []
-    for i, (ref, joined) in enumerate(
-        ((up_own, up_ref), (up_other, up_ref), (down_own, down_ref), (down_other, down_ref))
-    ):
-        held = joined.at[pl.ds((i % 2) * features, features), :]
-        copies.append(pltpu.make_async_copy(ref, held, sems.at[i]))
-    for copy in copies:
-        copy.start()
-    groups = unpack_rows(split_tiles(recv_ref[...]), recv_ref.shape[0])
+    rows = pack_rows(rank_ref[...], gate_ref[...], source)
+    start = 0
+    for ref in out_refs:
+        ref[...] = rows[:, start : start + ref.shape[1]].astype(BF16)
+        start += ref.shape[1]
+
+
+def up_kernel(up_own, up_other, down_own, down_other, *refs):
+    *recv, out_ref, x_ref, dy_ref = refs
+    tiles = [tile for ref in recv for tile in split_tiles(ref[...])]
+    groups = unpack_rows(tiles, recv[0].shape[0])
     for g in range(7):
         x_ref[:, g * 128 : (g + 1) * 128] = groups[g].astype(BF16)
         dy_ref[:, g * 128 : (g + 1) * 128] = groups[7 + g].astype(BF16)
     rows = x_ref.shape[0]
     block = out_ref.shape[2]
-    for n, (lhs, joined) in enumerate(((x_ref, up_ref), (dy_ref, down_ref))):
-        copies[2 * n].wait()
-        copies[2 * n + 1].wait()
-        for q in range(out_ref.shape[0]):
-            units = slice(q * block, (q + 1) * block)
-            part = dot(lhs[...], joined[:, units], ((1,), (0,)))
-            out_ref[q, n * rows : (n + 1) * rows, :] = part.astype(BF16)
+    for q in range(out_ref.shape[0]):
+        units = slice(q * block, (q + 1) * block)
+        up = jnp.concatenate([up_own[:, units], up_other[:, units]], axis=0)
+        down = jnp.concatenate([down_own[:, units], down_other[:, units]], axis=0)
+        out_ref[q, :rows, :] = dot(x_ref[...], up, ((1,), (0,))).astype(BF16)
+        out_ref[q, rows:, :] = dot(dy_ref[...], down, ((1,), (0,))).astype(BF16)
 
 
 def act_kernel(parts_ref, out_ref):
@@ -187,17 +183,19 @@
         out_ref[q, 1] = dpre
 
 
-def down_kernel(recv_ref, up_ref, down_ref, out_ref):
+def down_kernel(recv_ref, up_own, up_other, down_own, down_other, out_ref):
     chips, rows, _ = recv_ref.shape
     half = rows // 2
-    features = up_ref.shape[0]
+    features = up_own.shape[0]
+    even = features // 128 * 128
+    odd = features - even
     groups = []
-    for first, weight_ref in ((0, down_ref), (half, up_ref)):
+    for first, own, other in ((0, down_own, down_other), (half, up_own, up_other)):
         acts = jnp.concatenate([recv_ref[q, first : first + half, :] for q in range(chips)], axis=1)
-        for start in range(0, features, 256):
-            stop = min(start + 256, features)
-            out = dot(acts, weight_ref[start:stop, :], ((1,), (1,))).astype(BF16)
-            groups += [out[:, n : n + 128] for n in range(0, stop - start, 128)]
+        between = jnp.concatenate([own[even:, :], other[: 128 - odd, :]], axis=0)
+        for weight in (own[:even, :], between, other[128 - odd :, :]):
+            out = dot(acts, weight, ((1,), (1,))).astype(BF16)
+            groups += [out[:, n : n + 128] for n in range(0, out.shape[1], 128)]
     out_ref[...] = repack_rows(groups, out_ref.shape[0]).astype(BF16)
 
 
@@ -210,19 +208,18 @@
     other_ref[1] = grad[width:].astype(BF16)
 
 
-def in_vmem(kernel, name, outs, operands, far=(), scratch=(), mebibytes=16):
+def in_vmem(kernel, name, outs, operands, scratch=()):
     vmem = pl.BlockSpec(memory_space=pltpu.VMEM)
     scalar = pl.BlockSpec(memory_space=pltpu.SMEM)
-    hbm = pl.BlockSpec(memory_space=pltpu.HBM)
     return pl.pallas_call(
         kernel,
         out_shape=outs,
-        in_specs=[scalar if x.size == 1 else vmem for x in operands] + [hbm] * len(far),
+        in_specs=[scalar if x.size == 1 else vmem for x in operands],
         out_specs=jax.tree.map(lambda _: vmem, outs),
         scratch_shapes=list(scratch),
-        compiler_params=pltpu.CompilerParams(vmem_limit_bytes=mebibytes * 1024 * 1024),
+        compiler_params=pltpu.CompilerParams(vmem_limit_bytes=16 * 1024 * 1024),
         name=name,
-    )(*operands, *far)
+    )(*operands)
 
 
 def local(tokens, grad_out, expert_ids, route_weight, up_weight, down_weight):
@@ -257,46 +254,47 @@
     up_other = lax.ppermute(up_own, "section", swap)
     down_other = lax.ppermute(down_own, "section", swap)
 
-    def at_once(rows):
-        return across_experts(rows)
-
-    def in_two(rows):
-        return jnp.concatenate([across_experts(rows[:, :LEAD]), across_experts(rows[:, LEAD:])], axis=1)
-
-    send = in_vmem(send_kernel, "send_rows", message, (rank, gate, own, other))
-    recv = lax.cond(core[0, 0] == 0, at_once, in_two, send)
-
-    joined = jax.ShapeDtypeStruct((2 * features, hidden_units), BF16)
-    parts, up_both, down_both = in_vmem(
-        up_kernel,
-        "up_products",
-        (parts_type, joined, joined),
-        (recv,),
-        (up_own, up_other, down_own, down_other),
-        [pltpu.VMEM((rows, 2 * features), BF16)] * 2 + [pltpu.SemaphoreType.DMA((4,))],
-        44,
-    )
-    parts = across_chips(parts)
+    weights = (up_own, up_other, down_own, down_other)
     steps = 4
     act_spec = pl.BlockSpec((chips, 2, rows // steps, block), lambda i: (0, 0, i, 0))
-    acts = pl.pallas_call(
-        act_kernel,
-        grid=(steps,),
-        out_shape=jax.ShapeDtypeStruct((chips, 2, rows, block), BF16),
-        in_specs=[act_spec],
-        out_specs=act_spec,
-        compiler_params=pltpu.CompilerParams(vmem_limit_bytes=16 * 1024 * 1024),
-        name="activations",
-    )(parts.reshape(chips, 2, rows, block))
-    acts = across_chips(acts.reshape(chips, 2 * rows, block))
-    back = across_experts(in_vmem(down_kernel, "down_products", message, (acts, up_both, down_both)))
-
     own_sum = jax.ShapeDtypeStruct((features, tok_count), F32)
-    mixed, grad, rest = in_vmem(
-        combine_kernel,
-        "combine_rows",
-        (own_sum, own_sum, jax.ShapeDtypeStruct((2, features, tok_count), BF16)),
-        (rank, gate, back),
+    sums = (own_sum, own_sum, jax.ShapeDtypeStruct((2, features, tok_count), BF16))
+
+    def layer(lead, rank, gate, own, other, *weights):
+        cuts = [0, lead, 8 * TILES] if lead else [0, 8 * TILES]
+        kinds = tuple(
+            jax.ShapeDtypeStruct((experts, stop - start, 128), BF16) for start, stop in zip(cuts, cuts[1:])
+        )
+        recv = [across_experts(x) for x in in_vmem(send_kernel, "send_rows", kinds, (rank, gate, own, other))]
+        parts = in_vmem(
+            up_kernel,
+            "up_products",
+            parts_type,
+            (*weights, *recv),
+            [pltpu.VMEM((rows, 2 * features), BF16)] * 2,
+        )
+        acts = pl.pallas_call(
+            act_kernel,
+            grid=(steps,),
+            out_shape=jax.ShapeDtypeStruct((chips, 2, rows, block), BF16),
+            in_specs=[act_spec],
+            out_specs=act_spec,
+            compiler_params=pltpu.CompilerParams(vmem_limit_bytes=16 * 1024 * 1024),
+            name="activations",
+        )(across_chips(parts).reshape(chips, 2, rows, block))
+        acts = across_chips(acts.reshape(chips, 2 * rows, block))
+        back = across_experts(in_vmem(down_kernel, "down_products", message, (acts, *weights)))
+        return in_vmem(combine_kernel, "combine_rows", sums, (rank, gate, back))
+
+    mixed, grad, rest = lax.cond(
+        core[0, 0] == 0,
+        functools.partial(layer, 0),
+        functools.partial(layer, LEAD),
+        rank,
+        gate,
+        own,
+        other,
+        *weights,
     )
     rest = lax.ppermute(rest, "section", swap).astype(F32)
     return (mixed + rest[0]).astype(BF16).T, (grad + rest[1]).astype(BF16).T

time: 166 us -> 163 us (0.982)
  blocking collectives: 102 us -> 130 us
  waiting for transfers between devices: 19.1 us -> 1.79 us
  starting transfers between devices: 27.5 us -> 15 us
  local copies, waits for them, and re-layouts: 3.58 us -> 1.41 us
    all_to_all x2 -> x3, blocking collectives: 59.5 us -> 90.1 us  [across_experts(): return lax.all_to_all(x, 'expert', split_axis=0, concat_axis=0, tiled=True)]
    all_to_all x1 -> x0, waiting for transfers between devices: 17.3 us -> none  [across_experts(): return lax.all_to_all(x, 'expert', split_axis=0, concat_axis=0, tiled=True)]
    all_to_all x1 -> x0, starting transfers between devices: 12.5 us -> none  [across_experts(): return lax.all_to_all(x, 'expert', split_axis=0, concat_axis=0, tiled=True)]
    all_to_all x2, blocking collectives: 42.2 us -> 39.9 us  [across_chips(): lax.all_to_all(x, 'section', split_axis=0, concat_axis=0, axis_index_grou...]
  transfers between devices with their start and end apart: 5 -> 4, of which waited for: 2 -> 1; matrix products, arithmetic and copies ran while one was open for 1% -> 1% of each run, Pallas kernels for 0% -> 0%
where the time goes in v3:
time: 163 us; the launch traced here: 162 us
  blocking collectives  130 us (80%)
  starting transfers between devices  15 us (9%)
  Pallas kernels  11.1 us (7%)
  other arithmetic  2 us (1%)
  waiting for transfers between devices  1.79 us (1%)
    all_to_all x3, blocking collectives, across_experts(): return lax.all_to_all(x, 'expert', split_axis=0, concat_axis=0, tiled=True)  90.1 us
    all_to_all x2, blocking collectives, across_chips(): lax.all_to_all(x, 'section', split_axis=0, concat_axis=0, axis_index_grou...  39.9 us
    pallas_call x5, Pallas kernels, in_vmem(): pl.pallas_call(kernel, out_shape=outs, in_specs=[scalar if x.size == 1 el...  10.6 us
    ppermute x1, starting transfers between devices, local(): up_other = lax.ppermute(up_own, 'section', swap)  8.79 us
  transfers between devices with their start and end apart: 4, of which 1 were waited for; matrix products, arithmetic and copies ran while one was open for 1% of the time, Pallas kernels for 0%

profile of v3, /device:TPU:1, one launch (start us, length us, event | category | flops | bytes accessed | tf_op | source)
XLA Modules:
  0.0 162.5 jit_solution(991836513530281832)
XLA Ops:
  0.6 8.8 %collective-permute-start.1 = (bf16[448,2048]{1,0:T(8,128)(2,1)}, bf16[448,2048]{1,0:T(8,128)(2,1)S(1)}, u32[]{:S(2)}, u32[]{:S(2)}) collective-permute-start(bf16[448,2048]{1,0:T(8,128)(2,1)} %bitcast.39), channel_id=1, source_target_pairs={{0,32},{32,0},{64,96},{96,64},{128,160},{160,128},{192,224},{224,1... | collective-permute-start | bytes 5505032 | tf_op jit(solution)/shard_map/ppermute | solution.py:254
  9.4 1.9 %collective-permute-start.2 = (bf16[448,2048]{1,0:T(8,128)(2,1)}, bf16[448,2048]{1,0:T(8,128)(2,1)}, u32[]{:S(2)}, u32[]{:S(2)}) collective-permute-start(bf16[448,2048]{1,0:T(8,128)(2,1)} %bitcast.42), channel_id=1, source_target_pairs={{0,32},{32,0},{64,96},{96,64},{128,160},{160,128},{192,224},{224,1... | collective-permute-start | bytes 5505032 | tf_op jit(solution)/shard_map/ppermute | solution.py:255
  11.4 1.1 pad_maximum_fusion
  12.4 2.4 %collective-permute-start = (bf16[896,256]{1,0:T(8,128)(2,1)S(1)}, bf16[896,256]{1,0:T(8,128)(2,1)S(1)}, u32[]{:S(2)}, u32[]{:S(2)}) collective-permute-start(bf16[896,256]{1,0:T(8,128)(2,1)S(1)} %pad_maximum_fusion), channel_id=1, source_target_pairs={{0,32},{32,0},{64,96},{96,64},{128,160},{160,128},{192,224},{224,1... | collective-permute-start | bytes 1376264 | tf_op jit(solution)/shard_map/ppermute | solution.py:249
  14.9 0.7 copy-done
  15.6 0.7 copy-done.1
  16.3 0.2 route.1
  16.5 141.4 %conditional.1 = ((f32[448,256]{1,0:T(8,128)S(1)}, f32[448,256]{1,0:T(8,128)S(1)}, bf16[2,448,256]{2,1,0:T(8,128)(2,1)S(1)})) conditional(s32[]{:T(128)} %convert_element_type.12, (f32[32,256]{1,0:T(8,128)S(1)}, f32[32,256]{1,0:T(8,128)S(1)}, bf16[896,256]{1,0:T(8,128)(2,1)S(1)}, bf16[896,256]{1,0:T(8,128)(2,1)S(1)}, bf16[448,2048]{1,0:T(8,128)(2,1)}, ...), branch_computations={%region_0.0_spmd, %region_1.0_spmd} | conditional | bytes 38535288 | solution.py:289
  16.5 0.0 copy-start.2
  16.5 0.6 send_rows.2
  17.1 26.9 %all_to_all.36.refs_0_ = bf16[32,8,128]{2,1,0:T(8,128)(2,1)S(1)} all-to-all(bf16[32,8,128]{2,1,0:T(8,128)(2,1)S(1)} %get-tuple-element.40), channel_id=1, replica_groups=mesh['section'=16,'expert'=32] {'expert'}, dimensions={0} | all-to-all | bytes 131072 | tf_op jit(solution)/shard_map/cond/branch_0_fun/all_to_all | solution.py:241
  44.1 29.2 %all_to_all.37.refs_1_ = bf16[32,80,128]{2,1,0:T(8,128)(2,1)S(1)} all-to-all(bf16[32,80,128]{2,1,0:T(8,128)(2,1)S(1)} %get-tuple-element.41), channel_id=1, replica_groups=mesh['section'=16,'expert'=32] {'expert'}, dimensions={0} | all-to-all | bytes 1310720 | tf_op jit(solution)/shard_map/cond/branch_0_fun/all_to_all | solution.py:241
  73.3 4.2 %up_products.2 = bf16[8,384,256]{2,1,0:T(8,128)(2,1)S(1)} custom-call(bf16[448,2048]{1,0:T(8,128)(2,1)S(1)} %copy-done.2, bf16[448,2048]{1,0:T(8,128)(2,1)S(1)} %get-tuple-element.35.up_other, bf16[448,2048]{1,0:T(8,128)(2,1)} %get-tuple-element.36.down_own, bf16[448,2048]{1,0:T(8,128)(2,1)} %get-tuple-element.37.down_other, ...), custom_call_target="tpu_custom_call" | custom-call | tf_op jit(solution)/shard_map/cond/branch_0_fun/up_products/pallas_call | solution.py:214
  77.5 24.0 %all_to_all.38 = bf16[8,384,256]{2,1,0:T(8,128)(2,1)S(1)} all-to-all(bf16[8,384,256]{2,1,0:T(8,128)(2,1)S(1)} %up_products.2), channel_id=1, replica_groups={{0,64,128,192,256,320,384,448},{32,96,160,224,288,352,416,480},{1,65,12..., dimensions={0} | all-to-all | bytes 3145728 | tf_op jit(solution)/shard_map/cond/branch_0_fun/all_to_all | solution.py:244
  101.6 0.6 activations.2
  102.1 0.0 copy-start.4
  102.1 15.9 %all_to_all.39.recv_ref = bf16[8,384,256]{2,1,0:T(8,128)(2,1)S(1)} all-to-all(bf16[8,384,256]{2,1,0:T(8,128)(2,1)S(1)} %bitcast.34), channel_id=1, replica_groups={{0,64,128,192,256,320,384,448},{32,96,160,224,288,352,416,480},{1,65,12..., dimensions={0} | all-to-all | bytes 3145728 | tf_op jit(solution)/shard_map/cond/branch_0_fun/all_to_all | solution.py:244
  118.1 4.6 %down_products.2 = bf16[32,88,128]{2,1,0:T(8,128)(2,1)S(1)} custom-call(bf16[8,384,256]{2,1,0:T(8,128)(2,1)S(1)} %all_to_all.39.recv_ref, bf16[448,2048]{1,0:T(8,128)(2,1)S(1)} %copy-done.2, bf16[448,2048]{1,0:T(8,128)(2,1)S(1)} %copy-done.7, bf16[448,2048]{1,0:T(8,128)(2,1)S(1)} %copy-done.4, bf16[448,2048]{1,0:T(8,128)(2,1)} %get-tuple-element.37.down_other), custom_call_target="tpu_custom_call" | custom-call | tf_op jit(solution)/shard_map/cond/branch_0_fun/down_products/pallas_call | solution.py:214
  122.7 34.0 %all_to_all.40.recv_ref = bf16[32,88,128]{2,1,0:T(8,128)(2,1)S(1)} all-to-all(bf16[32,88,128]{2,1,0:T(8,128)(2,1)S(1)} %down_products.2), channel_id=1, replica_groups=mesh['section'=16,'expert'=32] {'expert'}, dimensions={0} | all-to-all | bytes 1441792 | tf_op jit(solution)/shard_map/cond/branch_0_fun/all_to_all | solution.py:241
  156.7 0.9 combine_rows.2
  157.8 1.9 %collective-permute-start.3 = (bf16[2,448,256]{2,1,0:T(8,128)(2,1)S(1)}, bf16[2,448,256]{2,1,0:T(8,128)(2,1)S(1)}, u32[]{:S(2)}, u32[]{:S(2)}) collective-permute-start(bf16[2,448,256]{2,1,0:T(8,128)(2,1)S(1)} %get-tuple-element.60), channel_id=1, source_target_pairs={{0,32},{32,0},{64,96},{96,64},{128,160},{160,128},{192,224},{224,1... | collective-permute-start | bytes 1376264 | tf_op jit(solution)/shard_map/ppermute | solution.py:299
  159.8 1.8 %collective-permute-done.3 = bf16[2,448,256]{2,1,0:T(8,128)(2,1)S(1)} collective-permute-done((bf16[2,448,256]{2,1,0:T(8,128)(2,1)S(1)}, bf16[2,448,256]{2,1,0:T(8,128)(2,1)S(1)}, u32[]{:S(2)}, u32[]{:S(2)}) %collective-permute-start.3) | collective-permute-done | bytes 458784 | tf_op jit(solution)/shard_map/ppermute | solution.py:299
  161.5 0.1 convert_element_type.13
  161.6 0.9 fusion.5
  (11 shorter events, 0.0 us)
Async XLA Ops:
  0.6 15.8 %collective-permute-start.1 = (bf16[448,2048]{1,0:T(8,128)(2,1)}, bf16[448,2048]{1,0:T(8,128)(2,1)S(1)}, u32[]{:S(2)}, u32[]{:S(2)}) collective-permute-start(bf16[448,2048]{1,0:T(8,128)(2,1)} %bitcast.39), channel_id=1, source_target_pairs={{0,32},{32,0},{64,96},{96,64},{128,160},{160,128},{192,224},{224,1... | collective-permute-start | bytes 5505032 | tf_op jit(solution)/shard_map/ppermute | solution.py:254
  9.4 7.0 %collective-permute-start.2 = (bf16[448,2048]{1,0:T(8,128)(2,1)}, bf16[448,2048]{1,0:T(8,128)(2,1)}, u32[]{:S(2)}, u32[]{:S(2)}) collective-permute-start(bf16[448,2048]{1,0:T(8,128)(2,1)} %bitcast.42), channel_id=1, source_target_pairs={{0,32},{32,0},{64,96},{96,64},{128,160},{160,128},{192,224},{224,1... | collective-permute-start | bytes 5505032 | tf_op jit(solution)/shard_map/ppermute | solution.py:255
  12.4 4.0 %collective-permute-start = (bf16[896,256]{1,0:T(8,128)(2,1)S(1)}, bf16[896,256]{1,0:T(8,128)(2,1)S(1)}, u32[]{:S(2)}, u32[]{:S(2)}) collective-permute-start(bf16[896,256]{1,0:T(8,128)(2,1)S(1)} %pad_maximum_fusion), channel_id=1, source_target_pairs={{0,32},{32,0},{64,96},{96,64},{128,160},{160,128},{192,224},{224,1... | collective-permute-start | bytes 1376264 | tf_op jit(solution)/shard_map/ppermute | solution.py:249
  14.9 0.7 copy-start
  15.6 0.7 copy-start.1
  16.5 61.1 %copy-start.6 = (bf16[448,2048]{1,0:T(8,128)(2,1)}, bf16[448,2048]{1,0:T(8,128)(2,1)S(1)}, u32[]{:S(2)}) copy-start(bf16[448,2048]{1,0:T(8,128)(2,1)S(1)} %get-tuple-element.35.up_other) | copy-start | bytes 5505028 | tf_op jit(solution)/shard_map/cond
  16.5 56.8 %copy-start.2 = (bf16[448,2048]{1,0:T(8,128)(2,1)S(1)}, bf16[448,2048]{1,0:T(8,128)(2,1)}, u32[]{:S(2)}) copy-start(bf16[448,2048]{1,0:T(8,128)(2,1)} %get-tuple-element.34.up_own) | copy-start | bytes 5505028 | tf_op jit(solution)/shard_map/cond
  101.6 16.5 %copy-start.7 = (bf16[448,2048]{1,0:T(8,128)(2,1)S(1)}, bf16[448,2048]{1,0:T(8,128)(2,1)}, u32[]{:S(2)}) copy-start(bf16[448,2048]{1,0:T(8,128)(2,1)} %copy-done.6) | copy-start | bytes 5505028 | tf_op jit(solution)/shard_map/cond
  102.1 15.9 %copy-start.4 = (bf16[448,2048]{1,0:T(8,128)(2,1)S(1)}, bf16[448,2048]{1,0:T(8,128)(2,1)}, u32[]{:S(2)}) copy-start(bf16[448,2048]{1,0:T(8,128)(2,1)} %get-tuple-element.36.down_own) | copy-start | bytes 5505028 | tf_op jit(solution)/shard_map/cond
  157.8 3.7 %collective-permute-start.3 = (bf16[2,448,256]{2,1,0:T(8,128)(2,1)S(1)}, bf16[2,448,256]{2,1,0:T(8,128)(2,1)S(1)}, u32[]{:S(2)}, u32[]{:S(2)}) collective-permute-start(bf16[2,448,256]{2,1,0:T(8,128)(2,1)S(1)} %get-tuple-element.60), channel_id=1, source_target_pairs={{0,32},{32,0},{64,96},{96,64},{128,160},{160,128},{192,224},{224,1... | collective-permute-start | bytes 1376264 | tf_op jit(solution)/shard_map/ppermute | solution.py:299

commit v4 on v3

--- a/solution.py
+++ b/solution.py
@@ -109,23 +109,26 @@
     return jnp.concatenate([t.reshape(blocks, 8, 128) for t in tiles], axis=1)
 
 
-def combine_rows(rank, gate, tiles):
+def combine_rows(rank, gate, tiles, start, stop):
     experts, tokens = rank.shape
     rank3 = jnp.broadcast_to(rank[:, None, :], (experts, 8, tokens))
     gate2 = jnp.broadcast_to(gate[:, None, :], (experts, 8, tokens)).reshape(experts * 8, tokens)
+    used = range(start // 128, (stop + 127) // 128)
     groups = [None] * 14
 
     def add(g, part):
         groups[g] = part if groups[g] is None else groups[g] + part
 
     for shift, tile, group in SHIFTS:
-        pairs = pairs_of(tile, group)
+        pairs = [(k, g) for k, g in pairs_of(tile, group) if g % 7 in used]
         onehot = placed(rank3, shift)
         weight = onehot * gate2
         high = weight.astype(BF16)
         low = (weight - high.astype(F32)).astype(BF16)
         for scaled in (True, False):
             some = [(k, g) for k, g in pairs if (g < 7) == scaled]
+            if not some:
+                continue
             stacked = jnp.concatenate([tiles[k] for k, _ in some], axis=1)
             if scaled:
                 sums = dot(stacked, high, ((0,), (0,))) + dot(stacked, low, ((0,), (0,)))
@@ -133,7 +136,9 @@
                 sums = dot(stacked, onehot.astype(BF16), ((0,), (0,)))
             for n, (_, g) in enumerate(some):
                 add(g, sums[n * 128 : (n + 1) * 128])
-    return jnp.concatenate(groups[:7], axis=0), jnp.concatenate(groups[7:], axis=0)
+    first = used[0] * 128
+    joined = (jnp.concatenate([groups[half + j] for j in used], axis=0) for half in (0, 7))
+    return tuple(x[start - first : stop - first] for x in joined)
 
 
 def route_kernel(core_ref, ids_ref, gates_ref, rank_ref, gate_ref):
@@ -199,13 +204,18 @@
     out_ref[...] = repack_rows(groups, out_ref.shape[0]).astype(BF16)
 
 
-def combine_kernel(rank_ref, gate_ref, recv_ref, mixed_ref, grad_ref, other_ref):
-    mixed, grad = combine_rows(rank_ref[...], gate_ref[...], split_tiles(recv_ref[...]))
+def combine_own_kernel(rank_ref, gate_ref, recv_ref, mixed_ref, grad_ref):
     width = mixed_ref.shape[0]
-    mixed_ref[...] = mixed[:width]
-    grad_ref[...] = grad[:width]
-    other_ref[0] = mixed[width:].astype(BF16)
-    other_ref[1] = grad[width:].astype(BF16)
+    mixed, grad = combine_rows(rank_ref[...], gate_ref[...], split_tiles(recv_ref[...]), 0, width)
+    mixed_ref[...] = mixed
+    grad_ref[...] = grad
+
+
+def combine_other_kernel(rank_ref, gate_ref, recv_ref, out_ref):
+    width = out_ref.shape[1]
+    sums = combine_rows(rank_ref[...], gate_ref[...], split_tiles(recv_ref[...]), width, 2 * width)
+    for n in range(2):
+        out_ref[n] = sums[n].astype(BF16)
 
 
 def in_vmem(kernel, name, outs, operands, scratch=()):
@@ -258,7 +268,7 @@
     steps = 4
     act_spec = pl.BlockSpec((chips, 2, rows // steps, block), lambda i: (0, 0, i, 0))
     own_sum = jax.ShapeDtypeStruct((features, tok_count), F32)
-    sums = (own_sum, own_sum, jax.ShapeDtypeStruct((2, features, tok_count), BF16))
+    sums = jax.ShapeDtypeStruct((2, features, tok_count), BF16)
 
     def layer(lead, rank, gate, own, other, *weights):
         cuts = [0, lead, 8 * TILES] if lead else [0, 8 * TILES]
@@ -283,10 +293,9 @@
             name="activations",
         )(across_chips(parts).reshape(chips, 2, rows, block))
         acts = across_chips(acts.reshape(chips, 2 * rows, block))
-        back = across_experts(in_vmem(down_kernel, "down_products", message, (acts, *weights)))
-        return in_vmem(combine_kernel, "combine_rows", sums, (rank, gate, back))
-
-    mixed, grad, rest = lax.cond(
+        return across_experts(in_vmem(down_kernel, "down_products", message, (acts, *weights)))
+
+    back = lax.cond(
         core[0, 0] == 0,
         functools.partial(layer, 0),
         functools.partial(layer, LEAD),
@@ -296,7 +305,9 @@
         other,
         *weights,
     )
-    rest = lax.ppermute(rest, "section", swap).astype(F32)
+    shares = (rank, gate, back)
+    rest = lax.ppermute(in_vmem(combine_other_kernel, "combine_other", sums, shares), "section", swap).astype(F32)
+    mixed, grad = in_vmem(combine_own_kernel, "combine_own", (own_sum, own_sum), shares)
     return (mixed + rest[0]).astype(BF16).T, (grad + rest[1]).astype(BF16).T
 
 

time: 163 us -> 163 us (level)
    pallas_call x5 -> x6, Pallas kernels: 10.6 us -> 11.1 us  [in_vmem(): pl.pallas_call(kernel, out_shape=outs, in_specs=[scalar if x.size == 1 el...]
  transfers between devices with their start and end apart: 4 -> 4, of which waited for: 1 -> 1; matrix products, arithmetic and copies ran while one was open for 1% -> 1% of each run, Pallas kernels for 0% -> 1%
where the time goes in v4:
time: 163 us; the launch traced here: 162 us
  blocking collectives  130 us (80%)
  starting transfers between devices  15 us (9%)
  Pallas kernels  11.6 us (7%)
  other arithmetic  2 us (1%)
    all_to_all x3, blocking collectives, across_experts(): return lax.all_to_all(x, 'expert', split_axis=0, concat_axis=0, tiled=True)  90.1 us
    all_to_all x2, blocking collectives, across_chips(): lax.all_to_all(x, 'section', split_axis=0, concat_axis=0, axis_index_grou...  39.9 us
    pallas_call x6, Pallas kernels, in_vmem(): pl.pallas_call(kernel, out_shape=outs, in_specs=[scalar if x.size == 1 el...  11.1 us
    ppermute x1, starting transfers between devices, local(): up_other = lax.ppermute(up_own, 'section', swap)  8.79 us
  transfers between devices with their start and end apart: 4, of which 1 were waited for; matrix products, arithmetic and copies ran while one was open for 1% of the time, Pallas kernels for 1%

profile of v4, /device:TPU:1, one launch (start us, length us, event | category | flops | bytes accessed | tf_op | source)
XLA Modules:
  0.0 162.1 jit_solution(2658376245219096116)
XLA Ops:
  0.6 8.8 %collective-permute-start.1 = (bf16[448,2048]{1,0:T(8,128)(2,1)}, bf16[448,2048]{1,0:T(8,128)(2,1)S(1)}, u32[]{:S(2)}, u32[]{:S(2)}) collective-permute-start(bf16[448,2048]{1,0:T(8,128)(2,1)} %bitcast.39), channel_id=1, source_target_pairs={{0,32},{32,0},{64,96},{96,64},{128,160},{160,128},{192,224},{224,1... | collective-permute-start | bytes 5505032 | tf_op jit(solution)/shard_map/ppermute | solution.py:264
  9.4 1.9 %collective-permute-start.2 = (bf16[448,2048]{1,0:T(8,128)(2,1)}, bf16[448,2048]{1,0:T(8,128)(2,1)}, u32[]{:S(2)}, u32[]{:S(2)}) collective-permute-start(bf16[448,2048]{1,0:T(8,128)(2,1)} %bitcast.42), channel_id=1, source_target_pairs={{0,32},{32,0},{64,96},{96,64},{128,160},{160,128},{192,224},{224,1... | collective-permute-start | bytes 5505032 | tf_op jit(solution)/shard_map/ppermute | solution.py:265
  11.4 1.1 pad_maximum_fusion
  12.4 2.4 %collective-permute-start = (bf16[896,256]{1,0:T(8,128)(2,1)S(1)}, bf16[896,256]{1,0:T(8,128)(2,1)S(1)}, u32[]{:S(2)}, u32[]{:S(2)}) collective-permute-start(bf16[896,256]{1,0:T(8,128)(2,1)S(1)} %pad_maximum_fusion), channel_id=1, source_target_pairs={{0,32},{32,0},{64,96},{96,64},{128,160},{160,128},{192,224},{224,1... | collective-permute-start | bytes 1376264 | tf_op jit(solution)/shard_map/ppermute | solution.py:259
  14.9 0.0 copy-start
  14.9 0.7 copy-done
  15.6 0.7 copy-done.1
  16.3 0.2 route.1
  16.5 140.3 %conditional.1 = (bf16[32,88,128]{2,1,0:T(8,128)(2,1)S(1)}) conditional(s32[]{:T(128)} %convert_element_type.12, (f32[32,256]{1,0:T(8,128)S(1)}, f32[32,256]{1,0:T(8,128)S(1)}, bf16[896,256]{1,0:T(8,128)(2,1)S(1)}, bf16[896,256]{1,0:T(8,128)(2,1)S(1)}, bf16[448,2048]{1,0:T(8,128)(2,1)}, /*index=5*/bf16[448,2048]{1,0:T(8,128)(2,1)S(1)}, ...), branch_computations={%region_0.0_spmd, %region_1.0_spmd} | conditional | bytes 38535288 | solution.py:298
  16.5 0.6 send_rows.2
  17.1 26.9 %all_to_all.36.refs_0_ = bf16[32,8,128]{2,1,0:T(8,128)(2,1)S(1)} all-to-all(bf16[32,8,128]{2,1,0:T(8,128)(2,1)S(1)} %get-tuple-element.43), channel_id=1, replica_groups=mesh['section'=16,'expert'=32] {'expert'}, dimensions={0} | all-to-all | bytes 131072 | tf_op jit(solution)/shard_map/cond/branch_0_fun/all_to_all | solution.py:251
  44.1 29.2 %all_to_all.37.refs_1_ = bf16[32,80,128]{2,1,0:T(8,128)(2,1)S(1)} all-to-all(bf16[32,80,128]{2,1,0:T(8,128)(2,1)S(1)} %get-tuple-element.44), channel_id=1, replica_groups=mesh['section'=16,'expert'=32] {'expert'}, dimensions={0} | all-to-all | bytes 1310720 | tf_op jit(solution)/shard_map/cond/branch_0_fun/all_to_all | solution.py:251
  73.3 4.2 %up_products.2 = bf16[8,384,256]{2,1,0:T(8,128)(2,1)S(1)} custom-call(bf16[448,2048]{1,0:T(8,128)(2,1)S(1)} %copy-done.2, bf16[448,2048]{1,0:T(8,128)(2,1)S(1)} %get-tuple-element.36.up_other, bf16[448,2048]{1,0:T(8,128)(2,1)} %get-tuple-element.37.down_own, bf16[448,2048]{1,0:T(8,128)(2,1)} %get-tuple-element.38.down_other, ...), custom_call_target="tpu_custom_call" | custom-call | tf_op jit(solution)/shard_map/cond/branch_0_fun/up_products/pallas_call | solution.py:224
  77.5 24.0 %all_to_all.38 = bf16[8,384,256]{2,1,0:T(8,128)(2,1)S(1)} all-to-all(bf16[8,384,256]{2,1,0:T(8,128)(2,1)S(1)} %up_products.2), channel_id=1, replica_groups={{0,64,128,192,256,320,384,448},{32,96,160,224,288,352,416,480},{1,65,12..., dimensions={0} | all-to-all | bytes 3145728 | tf_op jit(solution)/shard_map/cond/branch_0_fun/all_to_all | solution.py:254
  101.6 0.6 activations.2
  102.1 15.9 %all_to_all.39.recv_ref = bf16[8,384,256]{2,1,0:T(8,128)(2,1)S(1)} all-to-all(bf16[8,384,256]{2,1,0:T(8,128)(2,1)S(1)} %bitcast.34), channel_id=1, replica_groups={{0,64,128,192,256,320,384,448},{32,96,160,224,288,352,416,480},{1,65,12..., dimensions={0} | all-to-all | bytes 3145728 | tf_op jit(solution)/shard_map/cond/branch_0_fun/all_to_all | solution.py:254
  118.1 4.6 %down_products.2 = bf16[32,88,128]{2,1,0:T(8,128)(2,1)S(1)} custom-call(bf16[8,384,256]{2,1,0:T(8,128)(2,1)S(1)} %all_to_all.39.recv_ref, bf16[448,2048]{1,0:T(8,128)(2,1)S(1)} %copy-done.2, bf16[448,2048]{1,0:T(8,128)(2,1)S(1)} %copy-done.7, bf16[448,2048]{1,0:T(8,128)(2,1)S(1)} %copy-done.4, bf16[448,2048]{1,0:T(8,128)(2,1)} %get-tuple-element.38.down_other), custom_call_target="tpu_custom_call" | custom-call | tf_op jit(solution)/shard_map/cond/branch_0_fun/down_products/pallas_call | solution.py:224
  122.7 34.0 %all_to_all.40 = bf16[32,88,128]{2,1,0:T(8,128)(2,1)S(1)} all-to-all(bf16[32,88,128]{2,1,0:T(8,128)(2,1)S(1)} %down_products.2), channel_id=1, replica_groups=mesh['section'=16,'expert'=32] {'expert'}, dimensions={0} | all-to-all | bytes 1441792 | tf_op jit(solution)/shard_map/cond/branch_0_fun/all_to_all | solution.py:251
  156.7 0.7 combine_other.1
  157.4 1.9 %collective-permute-start.3 = (bf16[2,448,256]{2,1,0:T(8,128)(2,1)S(1)}, bf16[2,448,256]{2,1,0:T(8,128)(2,1)S(1)}, u32[]{:S(2)}, u32[]{:S(2)}) collective-permute-start(bf16[2,448,256]{2,1,0:T(8,128)(2,1)S(1)} %combine_other.1), channel_id=1, source_target_pairs={{0,32},{32,0},{64,96},{96,64},{128,160},{160,128},{192,224},{224,1... | collective-permute-start | bytes 1376264 | tf_op jit(solution)/shard_map/ppermute | solution.py:309
  159.3 0.7 combine_own.1
  160.0 1.1 collective-permute-done.3
  161.1 0.1 convert_element_type.13
  161.2 0.9 fusion.5
  (12 shorter events, 0.0 us)
Async XLA Ops:
  0.6 15.8 %collective-permute-start.1 = (bf16[448,2048]{1,0:T(8,128)(2,1)}, bf16[448,2048]{1,0:T(8,128)(2,1)S(1)}, u32[]{:S(2)}, u32[]{:S(2)}) collective-permute-start(bf16[448,2048]{1,0:T(8,128)(2,1)} %bitcast.39), channel_id=1, source_target_pairs={{0,32},{32,0},{64,96},{96,64},{128,160},{160,128},{192,224},{224,1... | collective-permute-start | bytes 5505032 | tf_op jit(solution)/shard_map/ppermute | solution.py:264
  9.4 7.0 %collective-permute-start.2 = (bf16[448,2048]{1,0:T(8,128)(2,1)}, bf16[448,2048]{1,0:T(8,128)(2,1)}, u32[]{:S(2)}, u32[]{:S(2)}) collective-permute-start(bf16[448,2048]{1,0:T(8,128)(2,1)} %bitcast.42), channel_id=1, source_target_pairs={{0,32},{32,0},{64,96},{96,64},{128,160},{160,128},{192,224},{224,1... | collective-permute-start | bytes 5505032 | tf_op jit(solution)/shard_map/ppermute | solution.py:265
  12.4 4.0 %collective-permute-start = (bf16[896,256]{1,0:T(8,128)(2,1)S(1)}, bf16[896,256]{1,0:T(8,128)(2,1)S(1)}, u32[]{:S(2)}, u32[]{:S(2)}) collective-permute-start(bf16[896,256]{1,0:T(8,128)(2,1)S(1)} %pad_maximum_fusion), channel_id=1, source_target_pairs={{0,32},{32,0},{64,96},{96,64},{128,160},{160,128},{192,224},{224,1... | collective-permute-start | bytes 1376264 | tf_op jit(solution)/shard_map/ppermute | solution.py:259
  14.9 0.7 copy-start
  15.6 0.7 copy-start.1
  16.5 61.1 %copy-start.6 = (bf16[448,2048]{1,0:T(8,128)(2,1)}, bf16[448,2048]{1,0:T(8,128)(2,1)S(1)}, u32[]{:S(2)}) copy-start(bf16[448,2048]{1,0:T(8,128)(2,1)S(1)} %get-tuple-element.36.up_other) | copy-start | bytes 5505028 | tf_op jit(solution)/shard_map/cond
  16.5 56.8 %copy-start.2 = (bf16[448,2048]{1,0:T(8,128)(2,1)S(1)}, bf16[448,2048]{1,0:T(8,128)(2,1)}, u32[]{:S(2)}) copy-start(bf16[448,2048]{1,0:T(8,128)(2,1)} %get-tuple-element.23.up_own) | copy-start | bytes 5505028 | tf_op jit(solution)/shard_map/cond
  101.6 16.5 %copy-start.7 = (bf16[448,2048]{1,0:T(8,128)(2,1)S(1)}, bf16[448,2048]{1,0:T(8,128)(2,1)}, u32[]{:S(2)}) copy-start(bf16[448,2048]{1,0:T(8,128)(2,1)} %copy-done.6) | copy-start | bytes 5505028 | tf_op jit(solution)/shard_map/cond
  102.1 15.9 %copy-start.4 = (bf16[448,2048]{1,0:T(8,128)(2,1)S(1)}, bf16[448,2048]{1,0:T(8,128)(2,1)}, u32[]{:S(2)}) copy-start(bf16[448,2048]{1,0:T(8,128)(2,1)} %get-tuple-element.37.down_own) | copy-start | bytes 5505028 | tf_op jit(solution)/shard_map/cond
  157.4 3.7 %collective-permute-start.3 = (bf16[2,448,256]{2,1,0:T(8,128)(2,1)S(1)}, bf16[2,448,256]{2,1,0:T(8,128)(2,1)S(1)}, u32[]{:S(2)}, u32[]{:S(2)}) collective-permute-start(bf16[2,448,256]{2,1,0:T(8,128)(2,1)S(1)} %combine_other.1), channel_id=1, source_target_pairs={{0,32},{32,0},{64,96},{96,64},{128,160},{160,128},{192,224},{224,1... | collective-permute-start | bytes 1376264 | tf_op jit(solution)/shard_map/ppermute | solution.py:309

commit v5 on v4

--- a/solution.py
+++ b/solution.py
@@ -265,8 +265,6 @@
     down_other = lax.ppermute(down_own, "section", swap)
 
     weights = (up_own, up_other, down_own, down_other)
-    steps = 4
-    act_spec = pl.BlockSpec((chips, 2, rows // steps, block), lambda i: (0, 0, i, 0))
     own_sum = jax.ShapeDtypeStruct((features, tok_count), F32)
     sums = jax.ShapeDtypeStruct((2, features, tok_count), BF16)
 
@@ -283,15 +281,8 @@
             (*weights, *recv),
             [pltpu.VMEM((rows, 2 * features), BF16)] * 2,
         )
-        acts = pl.pallas_call(
-            act_kernel,
-            grid=(steps,),
-            out_shape=jax.ShapeDtypeStruct((chips, 2, rows, block), BF16),
-            in_specs=[act_spec],
-            out_specs=act_spec,
-            compiler_params=pltpu.CompilerParams(vmem_limit_bytes=16 * 1024 * 1024),
-            name="activations",
-        )(across_chips(parts).reshape(chips, 2, rows, block))
+        kind = jax.ShapeDtypeStruct((chips, 2, rows, block), BF16)
+        acts = in_vmem(act_kernel, "activations", kind, (across_chips(parts).reshape(kind.shape),))
         acts = across_chips(acts.reshape(chips, 2 * rows, block))
         return across_experts(in_vmem(down_kernel, "down_products", message, (acts, *weights)))
 

time: 163 us -> 163 us (level)
    pallas_call x6 -> x7, Pallas kernels: 11.1 us -> 11.3 us  [in_vmem(): pl.pallas_call(kernel, out_shape=outs, in_specs=[scalar if x.size == 1 el...]
where the time goes in v5:
time: 163 us; the launch traced here: 162 us
  blocking collectives  130 us (80%)
  starting transfers between devices  15 us (9%)
  Pallas kernels  11.3 us (7%)
  other arithmetic  2 us (1%)
    all_to_all x3, blocking collectives, across_experts(): return lax.all_to_all(x, 'expert', split_axis=0, concat_axis=0, tiled=True)  90.1 us
    all_to_all x2, blocking collectives, across_chips(): lax.all_to_all(x, 'section', split_axis=0, concat_axis=0, axis_index_grou...  40.3 us
    pallas_call x7, Pallas kernels, in_vmem(): pl.pallas_call(kernel, out_shape=outs, in_specs=[scalar if x.size == 1 el...  11.3 us
    ppermute x1, starting transfers between devices, local(): up_other = lax.ppermute(up_own, 'section', swap)  8.79 us
  transfers between devices with their start and end apart: 4, of which 1 were waited for; matrix products, arithmetic and copies ran while one was open for 1% of the time, Pallas kernels for 1%

profile of v5, /device:TPU:1, one launch (start us, length us, event | category | flops | bytes accessed | tf_op | source)
XLA Modules:
  0.0 162.1 jit_solution(4331069533953842204)
XLA Ops:
  0.6 8.8 %collective-permute-start.1 = (bf16[448,2048]{1,0:T(8,128)(2,1)}, bf16[448,2048]{1,0:T(8,128)(2,1)S(1)}, u32[]{:S(2)}, u32[]{:S(2)}) collective-permute-start(bf16[448,2048]{1,0:T(8,128)(2,1)} %bitcast.39), channel_id=1, source_target_pairs={{0,32},{32,0},{64,96},{96,64},{128,160},{160,128},{192,224},{224,1... | collective-permute-start | bytes 5505032 | tf_op jit(solution)/shard_map/ppermute | solution.py:264
  9.4 1.9 %collective-permute-start.2 = (bf16[448,2048]{1,0:T(8,128)(2,1)}, bf16[448,2048]{1,0:T(8,128)(2,1)}, u32[]{:S(2)}, u32[]{:S(2)}) collective-permute-start(bf16[448,2048]{1,0:T(8,128)(2,1)} %bitcast.42), channel_id=1, source_target_pairs={{0,32},{32,0},{64,96},{96,64},{128,160},{160,128},{192,224},{224,1... | collective-permute-start | bytes 5505032 | tf_op jit(solution)/shard_map/ppermute | solution.py:265
  11.4 1.1 pad_maximum_fusion
  12.4 2.4 %collective-permute-start = (bf16[896,256]{1,0:T(8,128)(2,1)S(1)}, bf16[896,256]{1,0:T(8,128)(2,1)S(1)}, u32[]{:S(2)}, u32[]{:S(2)}) collective-permute-start(bf16[896,256]{1,0:T(8,128)(2,1)S(1)} %pad_maximum_fusion), channel_id=1, source_target_pairs={{0,32},{32,0},{64,96},{96,64},{128,160},{160,128},{192,224},{224,1... | collective-permute-start | bytes 1376264 | tf_op jit(solution)/shard_map/ppermute | solution.py:259
  14.9 0.0 copy-start
  14.9 0.7 copy-done
  15.6 0.7 copy-done.1
  16.3 0.2 route.1
  16.5 140.3 %conditional.1 = (bf16[32,88,128]{2,1,0:T(8,128)(2,1)S(1)}) conditional(s32[]{:T(128)} %convert_element_type.12, (f32[32,256]{1,0:T(8,128)S(1)}, f32[32,256]{1,0:T(8,128)S(1)}, bf16[896,256]{1,0:T(8,128)(2,1)S(1)}, bf16[896,256]{1,0:T(8,128)(2,1)S(1)}, bf16[448,2048]{1,0:T(8,128)(2,1)}, /*index=5*/bf16[448,2048]{1,0:T(8,128)(2,1)S(1)}, ...), branch_computations={%region_0.0_spmd, %region_1.0_spmd} | conditional | bytes 38535288 | solution.py:289
  16.5 0.6 send_rows.2
  17.1 26.9 %all_to_all.36.refs_0_ = bf16[32,8,128]{2,1,0:T(8,128)(2,1)S(1)} all-to-all(bf16[32,8,128]{2,1,0:T(8,128)(2,1)S(1)} %get-tuple-element.43), channel_id=1, replica_groups=mesh['section'=16,'expert'=32] {'expert'}, dimensions={0} | all-to-all | bytes 131072 | tf_op jit(solution)/shard_map/cond/branch_0_fun/all_to_all | solution.py:251
  44.1 29.2 %all_to_all.37.refs_1_ = bf16[32,80,128]{2,1,0:T(8,128)(2,1)S(1)} all-to-all(bf16[32,80,128]{2,1,0:T(8,128)(2,1)S(1)} %get-tuple-element.44), channel_id=1, replica_groups=mesh['section'=16,'expert'=32] {'expert'}, dimensions={0} | all-to-all | bytes 1310720 | tf_op jit(solution)/shard_map/cond/branch_0_fun/all_to_all | solution.py:251
  73.3 4.2 %up_products.2 = bf16[8,384,256]{2,1,0:T(8,128)(2,1)S(1)} custom-call(bf16[448,2048]{1,0:T(8,128)(2,1)S(1)} %copy-done.2, bf16[448,2048]{1,0:T(8,128)(2,1)S(1)} %get-tuple-element.36.up_other, bf16[448,2048]{1,0:T(8,128)(2,1)} %get-tuple-element.37.down_own, bf16[448,2048]{1,0:T(8,128)(2,1)} %get-tuple-element.38.down_other, ...), custom_call_target="tpu_custom_call" | custom-call | tf_op jit(solution)/shard_map/cond/branch_0_fun/up_products/pallas_call | solution.py:224
  77.5 24.2 %all_to_all.38 = bf16[8,384,256]{2,1,0:T(8,128)(2,1)S(1)} all-to-all(bf16[8,384,256]{2,1,0:T(8,128)(2,1)S(1)} %up_products.2), channel_id=1, replica_groups={{0,64,128,192,256,320,384,448},{32,96,160,224,288,352,416,480},{1,65,12..., dimensions={0} | all-to-all | bytes 3145728 | tf_op jit(solution)/shard_map/cond/branch_0_fun/all_to_all | solution.py:254
  101.7 0.3 activations.2
  102.0 16.1 %all_to_all.39.recv_ref = bf16[8,384,256]{2,1,0:T(8,128)(2,1)S(1)} all-to-all(bf16[8,384,256]{2,1,0:T(8,128)(2,1)S(1)} %bitcast.34), channel_id=1, replica_groups={{0,64,128,192,256,320,384,448},{32,96,160,224,288,352,416,480},{1,65,12..., dimensions={0} | all-to-all | bytes 3145728 | tf_op jit(solution)/shard_map/cond/branch_0_fun/all_to_all | solution.py:254
  118.1 4.6 %down_products.2 = bf16[32,88,128]{2,1,0:T(8,128)(2,1)S(1)} custom-call(bf16[8,384,256]{2,1,0:T(8,128)(2,1)S(1)} %all_to_all.39.recv_ref, bf16[448,2048]{1,0:T(8,128)(2,1)S(1)} %copy-done.2, bf16[448,2048]{1,0:T(8,128)(2,1)S(1)} %copy-done.7, bf16[448,2048]{1,0:T(8,128)(2,1)S(1)} %copy-done.4, bf16[448,2048]{1,0:T(8,128)(2,1)} %get-tuple-element.38.down_other), custom_call_target="tpu_custom_call" | custom-call | tf_op jit(solution)/shard_map/cond/branch_0_fun/down_products/pallas_call | solution.py:224
  122.7 34.0 %all_to_all.40 = bf16[32,88,128]{2,1,0:T(8,128)(2,1)S(1)} all-to-all(bf16[32,88,128]{2,1,0:T(8,128)(2,1)S(1)} %down_products.2), channel_id=1, replica_groups=mesh['section'=16,'expert'=32] {'expert'}, dimensions={0} | all-to-all | bytes 1441792 | tf_op jit(solution)/shard_map/cond/branch_0_fun/all_to_all | solution.py:251
  156.7 0.7 combine_other.1
  157.4 1.9 %collective-permute-start.3 = (bf16[2,448,256]{2,1,0:T(8,128)(2,1)S(1)}, bf16[2,448,256]{2,1,0:T(8,128)(2,1)S(1)}, u32[]{:S(2)}, u32[]{:S(2)}) collective-permute-start(bf16[2,448,256]{2,1,0:T(8,128)(2,1)S(1)} %combine_other.1), channel_id=1, source_target_pairs={{0,32},{32,0},{64,96},{96,64},{128,160},{160,128},{192,224},{224,1... | collective-permute-start | bytes 1376264 | tf_op jit(solution)/shard_map/ppermute | solution.py:300
  159.4 0.7 combine_own.1
  160.1 1.1 collective-permute-done.3
  161.2 0.1 convert_element_type.13
  161.2 0.9 fusion.5
  (12 shorter events, 0.0 us)
Async XLA Ops:
  0.6 15.8 %collective-permute-start.1 = (bf16[448,2048]{1,0:T(8,128)(2,1)}, bf16[448,2048]{1,0:T(8,128)(2,1)S(1)}, u32[]{:S(2)}, u32[]{:S(2)}) collective-permute-start(bf16[448,2048]{1,0:T(8,128)(2,1)} %bitcast.39), channel_id=1, source_target_pairs={{0,32},{32,0},{64,96},{96,64},{128,160},{160,128},{192,224},{224,1... | collective-permute-start | bytes 5505032 | tf_op jit(solution)/shard_map/ppermute | solution.py:264
  9.4 7.0 %collective-permute-start.2 = (bf16[448,2048]{1,0:T(8,128)(2,1)}, bf16[448,2048]{1,0:T(8,128)(2,1)}, u32[]{:S(2)}, u32[]{:S(2)}) collective-permute-start(bf16[448,2048]{1,0:T(8,128)(2,1)} %bitcast.42), channel_id=1, source_target_pairs={{0,32},{32,0},{64,96},{96,64},{128,160},{160,128},{192,224},{224,1... | collective-permute-start | bytes 5505032 | tf_op jit(solution)/shard_map/ppermute | solution.py:265
  12.4 4.0 %collective-permute-start = (bf16[896,256]{1,0:T(8,128)(2,1)S(1)}, bf16[896,256]{1,0:T(8,128)(2,1)S(1)}, u32[]{:S(2)}, u32[]{:S(2)}) collective-permute-start(bf16[896,256]{1,0:T(8,128)(2,1)S(1)} %pad_maximum_fusion), channel_id=1, source_target_pairs={{0,32},{32,0},{64,96},{96,64},{128,160},{160,128},{192,224},{224,1... | collective-permute-start | bytes 1376264 | tf_op jit(solution)/shard_map/ppermute | solution.py:259
  14.9 0.7 copy-start
  15.6 0.7 copy-start.1
  16.5 61.1 %copy-start.6 = (bf16[448,2048]{1,0:T(8,128)(2,1)}, bf16[448,2048]{1,0:T(8,128)(2,1)S(1)}, u32[]{:S(2)}) copy-start(bf16[448,2048]{1,0:T(8,128)(2,1)S(1)} %get-tuple-element.36.up_other) | copy-start | bytes 5505028 | tf_op jit(solution)/shard_map/cond
  16.5 56.8 %copy-start.2 = (bf16[448,2048]{1,0:T(8,128)(2,1)S(1)}, bf16[448,2048]{1,0:T(8,128)(2,1)}, u32[]{:S(2)}) copy-start(bf16[448,2048]{1,0:T(8,128)(2,1)} %get-tuple-element.23.up_own) | copy-start | bytes 5505028 | tf_op jit(solution)/shard_map/cond
  101.7 16.4 %copy-start.7 = (bf16[448,2048]{1,0:T(8,128)(2,1)S(1)}, bf16[448,2048]{1,0:T(8,128)(2,1)}, u32[]{:S(2)}) copy-start(bf16[448,2048]{1,0:T(8,128)(2,1)} %copy-done.6) | copy-start | bytes 5505028 | tf_op jit(solution)/shard_map/cond
  102.0 16.1 %copy-start.4 = (bf16[448,2048]{1,0:T(8,128)(2,1)S(1)}, bf16[448,2048]{1,0:T(8,128)(2,1)}, u32[]{:S(2)}) copy-start(bf16[448,2048]{1,0:T(8,128)(2,1)} %get-tuple-element.37.down_own) | copy-start | bytes 5505028 | tf_op jit(solution)/shard_map/cond
  157.4 3.7 %collective-permute-start.3 = (bf16[2,448,256]{2,1,0:T(8,128)(2,1)S(1)}, bf16[2,448,256]{2,1,0:T(8,128)(2,1)S(1)}, u32[]{:S(2)}, u32[]{:S(2)}) collective-permute-start(bf16[2,448,256]{2,1,0:T(8,128)(2,1)S(1)} %combine_other.1), channel_id=1, source_target_pairs={{0,32},{32,0},{64,96},{96,64},{128,160},{160,128},{192,224},{224,1... | collective-permute-start | bytes 1376264 | tf_op jit(solution)/shard_map/ppermute | solution.py:300
